TPU v7x, 128 devices: a whole 4x4x4 slice. The times are simulated.
128 devices in a mesh: replica: 8 (over z_lo, x), shard: 16 (over z_hi, y, core).
Axes of the slice: x: 4, y: 4, z: 4 (z_hi: 2, z_lo: 2; z = z_hi * 2 + z_lo), core: 2. Of those that a mesh axis runs over, the one named last changes fastest.
Arguments:
- tokens: bfloat16 [8, 4096, 12288], P('replica', 'shard'), may hold values from -6 to 6
- cotangent: bfloat16 [8, 4096, 12288], P('replica', 'shard'), may hold values from -6 to 6
- inner_up: float32 [8, 12288, 384], P('replica', 'shard'), may hold values from -5 to 5
- adam_first: float32 [8, 12288, 384], P('replica', 'shard'), may hold values from -4 to 4
- adam_second: float32 [8, 12288, 384], P('replica', 'shard'), may hold values from 0.05 to 2
- inner_down: bfloat16 [8, 12288, 384], P('replica', 'shard'), may hold values from -6 to 6
- down_accum: float32 [8, 12288, 384], P('replica', 'shard'), may hold values from -6 to 6
- anchor_up: float32 [12288, 384], P('shard'), may hold values from -5 to 5
- outer_momentum: float32 [12288, 384], P('shard'), may hold values from -4 to 4
Outputs:
- new_anchor: float32 [12288, 384], P('shard')
- new_momentum: float32 [12288, 384], P('shard')
- new_first: float32 [8, 12288, 384], P('replica', 'shard')
- new_second: float32 [8, 12288, 384], P('replica', 'shard')
- new_down_accum: float32 [8, 12288, 384], P('replica', 'shard')
All inputs are finite; a program needn't handle non-finite values.
Results may differ from a plain program's by a relative error of at most 0.015.
Values may be sent and summed in bfloat16 or wider, within the bound.
A program may use at most 128 MiB of HBM per device.

v0:
```python
import jax
import jax.numpy as jnp
from jax import lax
from jax.sharding import PartitionSpec as P

D = 12288
FFW = 384


beta_one = 0.8
beta_two = 0.95
inner_rate = 0.05
decay_rate = 0.1
adam_eps = 1e-08
adam_steps = 20
outer_mu = 0.9
outer_rate = 0.7


def activation(values):
    return jax.nn.gelu(values, approximate=True)


def on_device(
    tokens,
    cotangent,
    inner_up,
    adam_first,
    adam_second,
    inner_down,
    down_accum,
    anchor_up,
    outer_momentum,
):
    inputs = tokens[0]
    upstream_grad = cotangent[0]
    master_up = inner_up[0]
    down_bf = inner_down[0]
    scale_in = D ** (-0.5)
    scale_hid = FFW ** (-0.5)
    up_bf = master_up.astype(jnp.bfloat16)
    columns = inputs
    pre_sum = jnp.dot(
        columns,
        lax.all_gather(up_bf, "shard", axis=0, tiled=True),
        preferred_element_type=jnp.float32,
    )
    pre_act = pre_sum * scale_in
    columns = upstream_grad
    upstream = (
        jnp.dot(
            columns,
            lax.all_gather(down_bf, "shard", axis=0, tiled=True),
            preferred_element_type=jnp.float32,
        )
        * scale_hid
    )
    activated, pullback = jax.vjp(activation, pre_act)
    grad_pre = pullback(upstream)[0].astype(jnp.bfloat16)
    act_bf = activated.astype(jnp.bfloat16)
    columns = upstream_grad
    product = lax.dot_general(
        columns, act_bf, (((0,), (0,)), ((), ())), preferred_element_type=jnp.float32
    )
    new_down = down_accum[0] + lax.psum_scatter(
        (product * scale_hid).astype(jnp.bfloat16), "shard", scatter_dimension=0, tiled=True
    ).astype(jnp.float32)
    columns = inputs
    product = lax.dot_general(
        columns, grad_pre, (((0,), (0,)), ((), ())), preferred_element_type=jnp.float32
    )
    up_grad = lax.psum_scatter(
        (product * scale_in).astype(jnp.bfloat16), "shard", scatter_dimension=0, tiled=True
    ).astype(jnp.float32)
    new_first = beta_one * adam_first[0] + (1.0 - beta_one) * up_grad
    new_second = beta_two * adam_second[0] + (1.0 - beta_two) * up_grad * up_grad
    fix_one = 1.0 - beta_one**adam_steps
    fix_two = 1.0 - beta_two**adam_steps
    stepped = master_up - inner_rate * (
        new_first / fix_one / (jnp.sqrt(new_second / fix_two) + adam_eps) + decay_rate * master_up
    )
    pseudo_grad = (anchor_up - stepped).astype(jnp.bfloat16)
    replicas = lax.axis_size("replica")
    outer_mean = lax.psum(pseudo_grad, "replica").astype(jnp.float32) / replicas
    new_momentum = outer_mu * outer_momentum + outer_mean
    new_anchor = anchor_up - outer_rate * (outer_mean + outer_mu * new_momentum)
    new_anchor, new_momentum, new_first, new_second = (
        new_anchor,
        new_momentum,
        new_first,
        new_second,
    )
    return (new_anchor, new_momentum, new_first[None], new_second[None], new_down[None])


def solution(mesh):
    return jax.shard_map(
        on_device,
        mesh=mesh,
        in_specs=(
            P("replica", "shard", None),
            P("replica", "shard", None),
            P("replica", "shard", None),
            P("replica", "shard", None),
            P("replica", "shard", None),
            P("replica", "shard", None),
            P("replica", "shard", None),
            P("shard", None),
            P("shard", None),
        ),
        out_specs=(
            P("shard", None),
            P("shard", None),
            P("replica", "shard", None),
            P("replica", "shard", None),
            P("replica", "shard", None),
        ),
        check_vma=False,
    )
```

profile of v0, /device:TPU:0, one launch (start us, length us, event | category | flops | bytes accessed | tf_op | source)
XLA Modules:
  0.0 491.4 jit_solution(15769244928769809248)
XLA Ops:
  7.2 0.0 all-gather.4.cloned.1.call-start
  7.2 1.6 copy.14
  8.9 0.9 bitcast_convert_fusion
  9.7 0.0 all-gather.4.cloned.1.call-update
  9.8 0.0 all-gather.6.cloned.1.call-start
  9.8 0.7 all-gather.6.cloned.1.call-update
  10.5 0.0 reduce-scatter.3.cloned.1.call-start
  10.6 80.1 %all-gather.4.cloned.1.call-done = bf16[12288,384]{0,1:T(8,128)(2,1)} async-done(((bf16[768,384]{0,1:T(8,128)(2,1)}), bf16[12288,384]{0,1:T(8,128)(2,1)}) %all-gather.4.cloned.1.call-update) | async-done | bytes 9437200 | tf_op jit(solution)/shard_map/all_gather | solution.py:45
  90.7 10.5 %fusion.9 = f32[256,384]{1,0:T(8,128)S(1)} fusion(bf16[12288,384]{0,1:T(8,128)(2,1)} %all-gather.4.cloned.1.call-done, bf16[1,256,12288]{2,1,0:T(8,128)(2,1)} %param.9), kind=kOutput, calls=%fused_computation.13 | convolution fusion | flops 2416017408 | bytes 16121856 | tf_op jit(solution)/shard_map/dot_general | solution.py:43
  101.1 66.8 %all-gather.6.cloned.1.call-done = bf16[1,12288,384]{2,1,0:T(8,128)(2,1)} async-done(((bf16[1,768,384]{2,1,0:T(8,128)(2,1)}), bf16[1,12288,384]{2,1,0:T(8,128)(2,1)}) %all-gather.6.cloned.1.call-update) | async-done | bytes 9437200 | tf_op jit(solution)/shard_map/all_gather | solution.py:53
  168.0 9.1 %fusion.32 = bf16[256,384]{1,0:T(8,128)(2,1)S(1)} fusion(f32[256,384]{1,0:T(8,128)S(1)} %fusion.9, bf16[1,12288,384]{2,1,0:T(8,128)(2,1)} %all-gather.6.cloned.1.call-done, bf16[1,256,12288]{2,1,0:T(8,128)(2,1)} %param.10), kind=kOutput, calls=%fused_computation.39 | convolution fusion | flops 2417983488 | bytes 16318464 | tf_op jit(solution)/shard_map/dot_general | solution.py:51
  177.1 9.1 %fusion = bf16[12288,384]{0,1:T(8,128)(2,1)} fusion(bf16[256,384]{1,0:T(8,128)(2,1)S(1)} %fusion.32, bf16[1,256,12288]{2,1,0:T(8,128)(2,1)} %param.9), kind=kOutput, calls=%fused_computation.2 | convolution fusion | flops 2425356288 | bytes 15925248 | tf_op jit(solution)/shard_map/dot_general | solution.py:69
  186.2 0.0 reduce-scatter.3.cloned.1.call-update
  186.2 0.2 reduce-scatter.5.cloned.1.call-start
  186.5 9.5 %fusion.1 = bf16[12288,384]{0,1:T(8,128)(2,1)} fusion(bf16[1,256,12288]{2,1,0:T(8,128)(2,1)} %param.10, f32[256,384]{1,0:T(8,128)S(1)} %fusion.9), kind=kOutput, calls=%fused_computation.3 | convolution fusion | flops 2426241024 | bytes 16121856 | tf_op jit(solution)/shard_map/dot_general | solution.py:62
  196.0 0.0 copy-start
  196.0 0.0 reduce-scatter.5.cloned.1.call-update
  196.0 0.0 all-reduce.2.cloned.1.call-start
  196.1 1.3 copy-done
  197.4 0.4 copy.19
  197.8 0.0 copy-start.1
  197.8 2.9 copy.15
  200.7 0.0 copy-done.1
  200.7 1.4 copy.16
  202.0 89.2 %reduce-scatter.3.cloned.1.call-done = bf16[768,384]{0,1:T(8,128)(2,1)} async-done(((bf16[12288,384]{0,1:T(8,128)(2,1)}), bf16[768,384]{0,1:T(8,128)(2,1)}) %reduce-scatter.3.cloned.1.call-update) | async-done | bytes 589840 | tf_op jit(solution)/shard_map/reduce_scatter | solution.py:72
  291.3 4.0 fusion.25
  295.3 0.0 all-reduce.2.cloned.1.call-update
  295.4 1.6 copy.18
  297.0 2.7 copy.20
  299.7 2.7 copy.23
  302.3 1.4 copy.24
  303.7 97.9 %reduce-scatter.5.cloned.1.call-done = bf16[768,384]{0,1:T(8,128)(2,1)} async-done(((bf16[12288,384]{0,1:T(8,128)(2,1)}), bf16[768,384]{0,1:T(8,128)(2,1)}) %reduce-scatter.5.cloned.1.call-update) | async-done | bytes 589840 | tf_op jit(solution)/shard_map/reduce_scatter | solution.py:65
  401.6 1.5 fusion.19
  403.1 1.4 copy.25
  404.5 73.9 %all-reduce.2.cloned.1.call-done = bf16[768,384]{0,1:T(8,128)(2,1)} async-done(((bf16[768,384]{0,1:T(8,128)(2,1)}), bf16[768,384]{0,1:T(8,128)(2,1)}) %all-reduce.2.cloned.1.call-update) | async-done | bytes 589840 | tf_op jit(solution)/shard_map/psum | solution.py:84
  478.5 2.4 multiply_add_fusion
  480.9 2.7 copy.21
  483.5 1.4 copy.22
Async XLA Ops:
  7.2 83.5 %all-gather.4.cloned.1.call-start = ((), (), s32[]{:S(2)}) async-start(), calls=%async_computation.2 | async-start | bytes 10027008 | tf_op jit(solution)/shard_map/all_gather | solution.py:45
  9.8 158.2 %all-gather.6.cloned.1.call-start = ((), (), s32[]{:S(2)}) async-start(), calls=%async_computation.6 | async-start | bytes 10027008 | tf_op jit(solution)/shard_map/all_gather | solution.py:53
  10.5 280.8 %reduce-scatter.3.cloned.1.call-start = ((), (), s32[]{:S(2)}) async-start(), calls=%async_computation.3 | async-start | bytes 10027008 | tf_op jit(solution)/shard_map/reduce_scatter | solution.py:72
  186.2 215.4 %reduce-scatter.5.cloned.1.call-start = ((), (), s32[]{:S(2)}) async-start(), calls=%async_computation.5 | async-start | bytes 10027008 | tf_op jit(solution)/shard_map/reduce_scatter | solution.py:65
  196.0 1.4 copy-start
  196.0 282.5 %all-reduce.2.cloned.1.call-start = ((), (), s32[]{:S(2)}) async-start(), calls=%async_computation.4 | async-start | bytes 1179648 | tf_op jit(solution)/shard_map/psum | solution.py:84
  197.8 2.9 copy-start.1
Sparse Core Ops, SparseCore 0:
  11.0 79.5 all-gather.3
  93.1 74.8 all-gather.5
  186.3 104.8 reduce-scatter.2
  295.6 106.0 reduce-scatter.4
  404.5 73.8 all-reduce.1
where the time goes:
time: 492 us; the launch traced here: 491 us
  waiting for transfers between devices  409 us (83%)
  matrix products  38.2 us (8%)
  local copies, waits for them, and re-layouts  21.4 us (4%)
  between operations  13.8 us (3%)
  other arithmetic  8.82 us (2%)
    reduce_scatter x1, waiting for transfers between devices, on_device(): lax.psum_scatter((product * scale_hid).astype(jnp.bfloat16), 'shard', sca...  97.9 us
    reduce_scatter x1, waiting for transfers between devices, on_device(): lax.psum_scatter((product * scale_in).astype(jnp.bfloat16), 'shard', scat...  89.2 us
    all_gather x1, waiting for transfers between devices, on_device(): lax.all_gather(up_bf, 'shard', axis=0, tiled=True)  80.1 us
    psum x1, waiting for transfers between devices, on_device(): outer_mean = lax.psum(pseudo_grad, 'replica').astype(jnp.float32) / replicas  73.9 us
    all_gather x1, waiting for transfers between devices, on_device(): lax.all_gather(down_bf, 'shard', axis=0, tiled=True)  66.8 us
    unnamed x15, local copies, waits for them, and re-layouts  21.4 us
    dot_general x1, matrix products, on_device(): jnp.dot(columns, lax.all_gather(up_bf, 'shard', axis=0, tiled=True), pref...  10.5 us
  transfers between devices with their start and end apart: 5, of which 5 were waited for; matrix products, arithmetic and copies ran while one was open for 8% of the time, Pallas kernels for 0%

commit v1 on v0

v1 whole, which is shorter than its diff:
```python
import jax
import jax.numpy as jnp
from jax import lax
from jax.experimental import pallas as pl
from jax.experimental.pallas import tpu as pltpu
from jax.sharding import PartitionSpec as P

MESH = pl.DeviceIdType.MESH
D = 12288
FFW = 384
TOK = 256
ROWS = 768
CH = 256
NCH = 3
HALF = CH // 2
HALF_F = FFW // 2
N_REP = 8
PIECE = CH // N_REP

beta_one = 0.8
beta_two = 0.95
inner_rate = 0.05
decay_rate = 0.1
adam_eps = 1e-08
adam_steps = 20
outer_mu = 0.9
outer_rate = 0.7
fix_one = 1.0 - beta_one**adam_steps
fix_two = 1.0 - beta_two**adam_steps
GELU_K = 0.7978845608028654
GELU_C = 0.044715

F_UP, F_M1, F_M2, F_ACC, F_ANC, F_MOM = range(6)


def kernel(
    tok, cot, up, m1, m2, dn, acc, anc, mom,
    o_anc, o_mom, o_m1, o_m2, o_acc,
    X, W, A, R, G, T, B, F, PS, PR, MN,
    load_sem, out_sem, x_sem, xs_sem, xr_sem, ags, agr, rss, rsr, ps, pr, gs, gr, ars, arr, mns, mnr,
):
    rep = lax.axis_index("replica")
    shd = lax.axis_index("shard")
    x, zl = rep % 4, rep // 4
    c, y, zh = shd % 2, (shd // 2) % 4, shd // 8

    def shard_at(dy, dz, core):
        return ((zh + dz) % 2) * 8 + ((y + dy) % 4) * 2 + core

    partner = (rep, shard_at(0, 0, 1 - c))
    yp = (rep, shard_at(1, 0, c))
    ym = (rep, shard_at(3, 0, c))
    zp = (rep, shard_at(0, 1, c))

    def peer(p):
        return ((zl + p // 4) % 2) * 4 + (x + p % 4) % 4

    peers = [(peer(p), shd) for p in range(N_REP)]

    local = []
    for i, ref in enumerate((up.at[0], m1.at[0], m2.at[0], acc.at[0], anc, mom)):
        local.append(pltpu.make_async_copy(ref, F.at[i], load_sem.at[i]))
    dn_load = pltpu.make_async_copy(dn.at[0], W.at[1, 0], load_sem.at[6])
    local[F_UP].start()
    dn_load.start()

    barrier = pltpu.get_barrier_semaphore()
    others = [partner, yp, ym, zp] + peers[1:]
    for other in others:
        pl.semaphore_signal(barrier, inc=1, device_id=other, device_id_type=MESH)

    x_local = [[], []]
    for w, src in enumerate((tok, cot)):
        for s in range(8):
            columns = pl.ds(pl.multiple_of(shard_at(s % 4, s // 4, c) * ROWS, ROWS), ROWS)
            copy = pltpu.make_async_copy(src.at[0, :, columns], X.at[w, s, pl.ds(0, TOK)], x_sem.at[w, s])
            copy.start()
            x_local[w].append(copy)

    local[F_UP].wait()
    W[0, 0] = F[F_UP].astype(jnp.bfloat16)
    dn_load.wait()
    pl.semaphore_wait(barrier, len(others))

    sends = []

    def send(src, dst, s_sem, r_sem, to):
        copy = pltpu.make_async_remote_copy(
            src_ref=src, dst_ref=dst, send_sem=s_sem, recv_sem=r_sem, device_id=to, device_id_type=MESH
        )
        copy.start()
        sends.append(copy)
        return copy

    ag = {}

    def ag_send(w, j, k, from_slot, to_slot, first, count, to):
        rows = pl.ds(j * CH + first, count)
        ag[w, j, k] = send(W.at[w, from_slot, rows], W.at[w, to_slot, rows], ags.at[w, j, k], agr.at[w, j, k], to)

    def ag_own_z(w, j):
        ag_send(w, j, 2, 0, 4, 0, CH, zp)

    def ag_own_y(w, j):
        ag_send(w, j, 0, 0, 3, 0, CH, yp)
        ag_send(w, j, 1, 0, 1, 0, CH, ym)

    def ag_half(w, j):
        ag[w, j, 0].wait_recv()
        ag_send(w, j, 5, 3, 2, 0, HALF, yp)
        ag[w, j, 1].wait_recv()
        ag_send(w, j, 6, 1, 2, HALF, HALF, ym)

    def ag_far(w, j):
        ag[w, j, 2].wait_recv()
        ag_send(w, j, 3, 4, 7, 0, CH, yp)
        ag_send(w, j, 4, 4, 5, 0, CH, ym)

    def ag_last(w, j):
        ag[w, j, 5].wait_recv()
        ag[w, j, 6].wait_recv()
        ag_send(w, j, 7, 2, 6, 0, CH, zp)

    def ag_end(w, j):
        for k in (3, 4, 7):
            ag[w, j, k].wait_recv()

    def forward(w, j, slots, first):
        rows = pl.ds(j * CH, CH)

        @pl.loop(0, 4)
        def _(t):
            at = pl.ds(pl.multiple_of(t * 128, 128), 128)
            total = None if first else A[w, at]
            for s in slots:
                part = jnp.dot(X[w, s, at, rows], W[w, s, rows], preferred_element_type=jnp.float32)
                total = part if total is None else total + part
            A[w, at] = total

    for j in range(NCH):
        ag_own_z(0, j)
        ag_own_y(0, j)

    x_send = [[], []]
    for w, src in enumerate((tok, cot)):
        for s in range(8):
            columns = pl.ds(pl.multiple_of(shard_at(s % 4, s // 4, 1 - c) * ROWS, ROWS), ROWS)
            x_send[w].append(
                send(src.at[0, :, columns], X.at[w, s, pl.ds(TOK, TOK)], xs_sem.at[w, s], xr_sem.at[w, s], partner)
            )

    for j in range(NCH):
        ag_own_z(1, j)
    ag_half(0, 0)
    ag_far(0, 0)
    for s in range(8):
        x_local[0][s].wait()
        x_send[0][s].wait_recv()
    forward(0, 0, (0, 1, 3, 4), True)
    ag_half(0, 1)
    ag_far(0, 1)
    forward(0, 1, (0, 1, 3, 4), False)
    ag_half(0, 2)
    ag_far(0, 2)
    for j in range(NCH):
        ag_own_y(1, j)
    for i in (F_M1, F_M2, F_ACC, F_ANC, F_MOM):
        local[i].start()
    forward(0, 2, (0, 1, 3, 4), False)
    ag_last(0, 0)
    ag_last(0, 1)
    ag_end(0, 0)
    forward(0, 0, (2, 5, 6, 7), False)
    ag_last(0, 2)
    ag_end(0, 1)
    forward(0, 1, (2, 5, 6, 7), False)
    for s in range(8):
        x_local[1][s].wait()
        x_send[1][s].wait_recv()
    ag_half(1, 0)
    ag_far(1, 0)
    ag_end(0, 2)
    forward(0, 2, (2, 5, 6, 7), False)

    def swap_partial(w):
        return send(A.at[w, pl.ds(TOK, TOK)], R.at[w], ps.at[w], pr.at[w], partner)

    def swap_hidden(w):
        return send(G.at[w, 0], G.at[w, 1], gs.at[w], gr.at[w], partner)

    def terms(w, j):
        rows = pl.ds(j * CH, CH)
        scale = D ** (-0.5) if w == 0 else FFW ** (-0.5)

        @pl.loop(0, 8)
        def _(s):
            part = jnp.dot(G[w, 0], X[w, s, pl.ds(0, TOK), rows], preferred_element_type=jnp.float32)
            part += jnp.dot(G[w, 1], X[w, s, pl.ds(TOK, TOK), rows], preferred_element_type=jnp.float32)
            T[w, j, s] = (part * scale).astype(jnp.bfloat16)

    partial = swap_partial(0)
    forward(1, 0, (0, 1, 3, 4), True)
    ag_half(1, 1)
    ag_far(1, 1)
    partial.wait_recv()

    @pl.loop(0, 2)
    def _(t):
        at = pl.ds(pl.multiple_of(t * 128, 128), 128)
        v = (A[0, at] + R[0, at]) * D ** (-0.5)
        R[0, at] = v
        act = 0.5 * v * (1.0 + jnp.tanh(GELU_K * (v + GELU_C * (v * v * v))))
        G[1, 0, :, at] = act.T.astype(jnp.bfloat16)

    hidden = swap_hidden(1)
    forward(1, 1, (0, 1, 3, 4), False)
    ag_half(1, 2)
    ag_far(1, 2)
    hidden.wait_recv()
    terms(1, 0)
    forward(1, 2, (0, 1, 3, 4), False)
    ag_last(1, 0)
    terms(1, 1)
    ag_last(1, 1)
    ag_end(1, 0)
    forward(1, 0, (2, 5, 6, 7), False)
    terms(1, 2)
    ag_last(1, 2)
    ag_end(1, 1)
    forward(1, 1, (2, 5, 6, 7), False)

    rs = {}

    def rs_send(w, j, k, src, dst, to):
        rs[w, j, k] = send(src, dst, rss.at[w, j, k], rsr.at[w, j, k], to)

    def rs_one(w, j):
        rs_send(w, j, 0, T.at[w, j, 6], B.at[w, j, 0], zp)
        rs_send(w, j, 1, T.at[w, j, 5], B.at[w, j, 1], yp)
        rs_send(w, j, 2, T.at[w, j, 7], B.at[w, j, 2], ym)

    def add(w, j, slot, rows, *held):
        total = T[w, j, slot, rows].astype(jnp.float32)
        for k in held:
            total += B[w, j, k, rows].astype(jnp.float32)
        T[w, j, slot, rows] = total.astype(jnp.bfloat16)

    low, high, full = pl.ds(0, HALF_F), pl.ds(HALF_F, HALF_F), pl.ds(0, FFW)

    def rs_two(w, j):
        rs[w, j, 0].wait_recv()
        add(w, j, 2, full, 0)
        rs_send(w, j, 3, T.at[w, j, 2, low], B.at[w, j, 3, low], yp)
        rs_send(w, j, 4, T.at[w, j, 2, high], B.at[w, j, 3, high], ym)
        rs[w, j, 1].wait_recv()
        rs[w, j, 2].wait_recv()
        add(w, j, 4, full, 1, 2)
        rs_send(w, j, 5, T.at[w, j, 4], B.at[w, j, 4], zp)

    def rs_three(w, j):
        rs[w, j, 3].wait_recv()
        add(w, j, 1, low, 3)
        rs_send(w, j, 6, T.at[w, j, 1], B.at[w, j, 5], yp)
        rs[w, j, 4].wait_recv()
        add(w, j, 3, high, 3)
        rs_send(w, j, 7, T.at[w, j, 3], B.at[w, j, 6], ym)

    def rs_four(w, j):
        for k in (5, 6, 7):
            rs[w, j, k].wait_recv()
        total = T[w, j, 0].astype(jnp.float32)
        for k in (4, 5, 6):
            total += B[w, j, k].astype(jnp.float32)
        return total.T

    rs_one(1, 0)
    ag_end(1, 2)
    forward(1, 2, (2, 5, 6, 7), False)
    partial = swap_partial(1)
    partial.wait_recv()

    @pl.loop(0, 2)
    def _(t):
        at = pl.ds(pl.multiple_of(t * 128, 128), 128)
        upstream = (A[1, at] + R[1, at]) * FFW ** (-0.5)
        v = R[0, at]
        squared = v * v
        th = jnp.tanh(GELU_K * (v + GELU_C * (v * squared)))
        slope = 0.5 * (1.0 + th) + 0.5 * v * (1.0 - th * th) * (GELU_K * (1.0 + 3.0 * GELU_C * squared))
        G[0, 0, :, at] = (upstream * slope).T.astype(jnp.bfloat16)

    hidden = swap_hidden(0)
    hidden.wait_recv()
    for j in range(NCH):
        terms(0, j)
        rs_one(0, j)
    rs_one(1, 1)
    rs_one(1, 2)
    rs_two(1, 0)
    for j in range(NCH):
        rs_two(0, j)
    rs_two(1, 1)
    rs_two(1, 2)
    for i in (F_M1, F_M2, F_ACC, F_ANC, F_MOM):
        local[i].wait()

    outs = []

    def put(i, ref, j):
        rows = pl.ds(j * CH, CH)
        copy = pltpu.make_async_copy(F.at[i, rows], ref.at[rows], out_sem.at[i - 1, j])
        copy.start()
        outs.append(copy)

    ar = {}

    def adam(j):
        rows = pl.ds(j * CH, CH)
        grad = rs_four(0, j)
        first = beta_one * F[F_M1, rows] + (1.0 - beta_one) * grad
        F[F_M1, rows] = first
        second = beta_two * F[F_M2, rows] + (1.0 - beta_two) * grad * grad
        F[F_M2, rows] = second
        master = F[F_UP, rows]
        stepped = master - inner_rate * (
            first / fix_one / (jnp.sqrt(second / fix_two) + adam_eps) + decay_rate * master
        )
        PS[j] = (F[F_ANC, rows] - stepped).astype(jnp.bfloat16)
        for p in range(1, N_REP):
            piece = pl.ds(pl.multiple_of(peers[p][0] * PIECE, PIECE), PIECE)
            back = (p // 4) * 4 + (-p) % 4
            ar[j, p] = send(PS.at[j, piece], PR.at[j, back], ars.at[j, p - 1], arr.at[j, back - 1], peers[p])
        put(F_M1, o_m1.at[0], j)
        put(F_M2, o_m2.at[0], j)

    mean = {}

    def reduce_mean(j):
        mine = pl.ds(pl.multiple_of(rep * PIECE, PIECE), PIECE)
        total = PS[j, mine].astype(jnp.float32)
        for p in range(1, N_REP):
            ar[j, p].wait_recv()
        for p in range(1, N_REP):
            total += PR[j, p].astype(jnp.float32)
        MN[j, mine] = (total / N_REP).astype(jnp.bfloat16)
        for p in range(1, N_REP):
            back = (p // 4) * 4 + (-p) % 4
            mean[j, p] = send(MN.at[j, mine], MN.at[j, mine], mns.at[j, p - 1], mnr.at[j, back - 1], peers[p])

    def outer(j):
        rows = pl.ds(j * CH, CH)
        for p in range(1, N_REP):
            mean[j, p].wait_recv()
        outer_mean = MN[j].astype(jnp.float32)
        new_momentum = outer_mu * F[F_MOM, rows] + outer_mean
        F[F_MOM, rows] = new_momentum
        F[F_ANC, rows] = F[F_ANC, rows] - outer_rate * (outer_mean + outer_mu * new_momentum)
        put(F_MOM, o_mom, j)
        put(F_ANC, o_anc, j)

    def down(j):
        rows = pl.ds(j * CH, CH)
        F[F_ACC, rows] = F[F_ACC, rows] + rs_four(1, j)
        put(F_ACC, o_acc.at[0], j)

    for j in range(NCH):
        rs_three(0, j)
    rs_three(1, 0)
    adam(0)
    rs_three(1, 1)
    adam(1)
    rs_three(1, 2)
    adam(2)
    for j in range(NCH):
        reduce_mean(j)
    down(0)
    down(1)
    for j in range(NCH):
        outer(j)
    down(2)
    for copy in sends:
        copy.wait_send()
    for copy in outs:
        copy.wait()


def on_device(tokens, cotangent, inner_up, adam_first, adam_second, inner_down, down_accum, anchor_up, outer_momentum):
    flat = jax.ShapeDtypeStruct((ROWS, FFW), jnp.float32)
    deep = jax.ShapeDtypeStruct((1, ROWS, FFW), jnp.float32)
    dma = pltpu.SemaphoreType.DMA
    bf16, f32 = jnp.bfloat16, jnp.float32
    return pl.pallas_call(
        kernel,
        out_shape=(flat, flat, deep, deep, deep),
        in_specs=[pl.BlockSpec(memory_space=pl.ANY)] * 9,
        out_specs=[pl.BlockSpec(memory_space=pl.ANY)] * 5,
        scratch_shapes=[
            pltpu.VMEM((2, 8, 2 * TOK, ROWS), bf16),
            pltpu.VMEM((2, 8, ROWS, FFW), bf16),
            pltpu.VMEM((2, 2 * TOK, FFW), f32),
            pltpu.VMEM((2, TOK, FFW), f32),
            pltpu.VMEM((2, 2, FFW, TOK), bf16),
            pltpu.VMEM((2, NCH, 8, FFW, CH), bf16),
            pltpu.VMEM((2, NCH, 7, FFW, CH), bf16),
            pltpu.VMEM((6, ROWS, FFW), f32),
            pltpu.VMEM((NCH, CH, FFW), bf16),
            pltpu.VMEM((NCH, N_REP, PIECE, FFW), bf16),
            pltpu.VMEM((NCH, CH, FFW), bf16),
            dma((7,)),
            dma((5, NCH)),
            dma((2, 8)),
            dma((2, 8)),
            dma((2, 8)),
            dma((2, NCH, 8)),
            dma((2, NCH, 8)),
            dma((2, NCH, 8)),
            dma((2, NCH, 8)),
            dma((2,)),
            dma((2,)),
            dma((2,)),
            dma((2,)),
            dma((NCH, N_REP - 1)),
            dma((NCH, N_REP - 1)),
            dma((NCH, N_REP - 1)),
            dma((NCH, N_REP - 1)),
        ],
        name="window",
        compiler_params=pltpu.CompilerParams(
            collective_id=0, has_side_effects=True, vmem_limit_bytes=58 * 2**20
        ),
        cost_estimate=pl.CostEstimate(flops=9_700_000_000, bytes_accessed=30_000_000, transcendentals=200_000),
    )(tokens, cotangent, inner_up, adam_first, adam_second, inner_down, down_accum, anchor_up, outer_momentum)


def solution(mesh):
    return jax.shard_map(
        on_device,
        mesh=mesh,
        in_specs=(
            P("replica", "shard", None),
            P("replica", "shard", None),
            P("replica", "shard", None),
            P("replica", "shard", None),
            P("replica", "shard", None),
            P("replica", "shard", None),
            P("replica", "shard", None),
            P("shard", None),
            P("shard", None),
        ),
        out_specs=(
            P("shard", None),
            P("shard", None),
            P("replica", "shard", None),
            P("replica", "shard", None),
            P("replica", "shard", None),
        ),
        check_vma=False,
    )
```

time: 492 us -> 160 us (0.33)
  waiting for transfers between devices: 409 us -> 0 us
  Pallas kernels: 0 us -> 151 us
  matrix products: 38.2 us -> 0 us
  between operations: 13.8 us -> 0.66 us
  local copies, waits for them, and re-layouts: 21.4 us -> 8.56 us
  other arithmetic: 8.82 us -> 0 us
    reduce_scatter x2 -> x0, waiting for transfers between devices: 187 us -> none  [the longest x1 97.9 us: on_device(): lax.psum_scatter((product * scale_hid).astype(jnp.bfloat16), 'shard', sca...]
    pallas_call x0 -> x1, Pallas kernels: none -> 151 us  [on_device(): pl.pallas_call(kernel, out_shape=(flat, flat, deep, deep, deep), in_specs...]
    all_gather x2 -> x0, waiting for transfers between devices: 147 us -> none  [the longest x1 80.1 us: on_device(): lax.all_gather(up_bf, 'shard', axis=0, tiled=True)]
    psum x1 -> x0, waiting for transfers between devices: 73.9 us -> none  [on_device(): outer_mean = lax.psum(pseudo_grad, 'replica').astype(jnp.float32) / replicas]
    dot_general x4 -> x0, matrix products: 38.2 us -> none  [the longest x1 10.5 us: on_device(): jnp.dot(columns, lax.all_gather(up_bf, 'shard', axis=0, tiled=True), pref...]
    unnamed x15 -> x13, local copies, waits for them, and re-layouts: 21.4 us -> 8.56 us
    broadcast_in_dim x2 -> x0, other arithmetic: 5.56 us -> none  [the longest x1 4.04 us: on_device(): new_second[None]]
  transfers between devices with their start and end apart: 5 -> 0, of which waited for: 5 -> 0; matrix products, arithmetic and copies ran while one was open for 8% -> 0% of each run, Pallas kernels for 0% -> 0%
where the time goes in v1:
time: 160 us
  Pallas kernels  151 us (94%)
  local copies, waits for them, and re-layouts  8.56 us (5%)
    pallas_call x1, Pallas kernels, on_device(): pl.pallas_call(kernel, out_shape=(flat, flat, deep, deep, deep), in_specs...  151 us
    unnamed x13, local copies, waits for them, and re-layouts  8.56 us

profile of v1, /device:TPU:0, one launch (start us, length us, event | category | flops | bytes accessed | tf_op | source)
XLA Modules:
  0.0 160.1 jit_solution(10967035367437249377)
XLA Ops:
  0.6 150.9 %window.1 = (f32[768,384]{1,0:T(8,128)}, f32[768,384]{1,0:T(8,128)}, f32[1,768,384]{2,1,0:T(8,128)}, f32[1,768,384]{2,1,0:T(8,128)}, f32[1,768,384]{2,1,0:T(8,128)}) custom-call(bf16[1,256,12288]{2,1,0:T(8,128)(2,1)} %tok.1, bf16[1,256,12288]{2,1,0:T(8,128)(2,1)} %cot.1, f32[1,768,384]{2,1,0:T(8,128)} %up.1, f32[1,768,384]{2,1,0:T(8,128)} %m1.1, ...), custom_call_target="tpu_custom_call" | custom-call | flops 9699999744 | bytes 30000000 | tf_op jit(solution)/shard_map/window/pallas_call | solution.py:392
  151.5 0.0 copy-start.3
  151.5 2.5 %copy.19 = f32[768,384]{1,0:T(8,128)} copy(f32[768,384]{1,0:T(8,128)} %get-tuple-element.10) | data formatting | bytes 2359296
  154.0 0.0 copy-done.3
  154.0 0.0 copy-start.2
  154.0 1.0 copy.20
  155.0 0.7 copy-done.2
  155.7 0.0 copy-start.1
  155.7 1.0 copy.21
  156.7 0.7 copy-done.1
  157.4 0.0 copy-start
  157.4 1.0 copy.22
  158.4 0.7 copy-done
  159.1 1.0 copy.23
Async XLA Ops:
  151.5 2.5 %copy-start.3 = (f32[768,384]{1,0:T(8,128)S(1)}, f32[768,384]{1,0:T(8,128)}, u32[]{:S(2)}) copy-start(f32[768,384]{1,0:T(8,128)} %get-tuple-element.11) | copy-start | bytes 3538948
  154.0 1.7 %copy-start.2 = (f32[1,768,384]{2,1,0:T(8,128)S(1)}, f32[1,768,384]{2,1,0:T(8,128)}, u32[]{:S(2)}) copy-start(f32[1,768,384]{2,1,0:T(8,128)} %get-tuple-element.12) | copy-start | bytes 3538948
  155.7 1.7 %copy-start.1 = (f32[1,768,384]{2,1,0:T(8,128)S(1)}, f32[1,768,384]{2,1,0:T(8,128)}, u32[]{:S(2)}) copy-start(f32[1,768,384]{2,1,0:T(8,128)} %get-tuple-element.13) | copy-start | bytes 3538948
  157.4 1.7 %copy-start = (f32[1,768,384]{2,1,0:T(8,128)S(1)}, f32[1,768,384]{2,1,0:T(8,128)}, u32[]{:S(2)}) copy-start(f32[1,768,384]{2,1,0:T(8,128)} %get-tuple-element.14) | copy-start | bytes 3538948

commit v2 on v1

v2 whole, which is shorter than its diff:
```python
import jax
import jax.numpy as jnp
from jax import lax
from jax.experimental import pallas as pl
from jax.experimental.pallas import tpu as pltpu
from jax.sharding import PartitionSpec as P

MESH = pl.DeviceIdType.MESH
D = 12288
FFW = 384
TOK = 256
ROWS = 768
CH = 256
NCH = 3
HALF = CH // 2
HALF_F = FFW // 2
N_REP = 8
PIECE = CH // N_REP
BY_Z_AG = (0,)
BY_Z_RS = ()

beta_one = 0.8
beta_two = 0.95
inner_rate = 0.05
decay_rate = 0.1
adam_eps = 1e-08
adam_steps = 20
outer_mu = 0.9
outer_rate = 0.7
fix_one = 1.0 - beta_one**adam_steps
fix_two = 1.0 - beta_two**adam_steps
GELU_K = 0.7978845608028654
GELU_C = 0.044715


def kernel(
    tok, cot, up, m1, m2, dn, acc, anc, mom,
    o_anc, o_mom, o_m1, o_m2, o_acc,
    X, W, A, R, G, T, B, U, PS, PR, MN,
    load_sem, x_sem, xs_sem, xr_sem, ags, agr, rss, rsr, ps, pr, gs, gr, ars, arr, mns, mnr,
):
    rep = lax.axis_index("replica")
    shd = lax.axis_index("shard")
    x, zl = rep % 4, rep // 4
    c, y, zh = shd % 2, (shd // 2) % 4, shd // 8

    def shard_at(dy, dz, core):
        return ((zh + dz) % 2) * 8 + ((y + dy) % 4) * 2 + core

    partner = (rep, shard_at(0, 0, 1 - c))
    yp = (rep, shard_at(1, 0, c))
    ym = (rep, shard_at(3, 0, c))
    zp = (rep, shard_at(0, 1, c))

    def peer(p):
        return ((zl + p // 4) % 2) * 4 + (x + p % 4) % 4

    peers = [(peer(p), shd) for p in range(N_REP)]

    barrier = pltpu.get_barrier_semaphore()
    others = [partner, yp, ym, zp] + peers[1:]
    for other in others:
        pl.semaphore_signal(barrier, inc=1, device_id=other, device_id_type=MESH)

    chunk = [pl.ds(j * CH, CH) for j in range(NCH)]
    up_load = [pltpu.make_async_copy(up.at[0, chunk[j]], U.at[chunk[j]], load_sem.at[j]) for j in range(NCH)]
    for copy in up_load:
        copy.start()
    dn_load = pltpu.make_async_copy(dn.at[0], W.at[1, 0], load_sem.at[3])
    late = [
        pltpu.make_async_copy(src, dst, load_sem.at[4 + i])
        for i, (src, dst) in enumerate(((m1.at[0], o_m1), (m2.at[0], o_m2), (acc.at[0], o_acc), (anc, o_anc), (mom, o_mom)))
    ]
    pl.semaphore_wait(barrier, len(others))

    sends = []

    def send(src, dst, s_sem, r_sem, to):
        copy = pltpu.make_async_remote_copy(
            src_ref=src, dst_ref=dst, send_sem=s_sem, recv_sem=r_sem, device_id=to, device_id_type=MESH
        )
        copy.start()
        sends.append(copy)
        return copy

    ag = {}

    def ag_send(w, j, k, from_slot, to_slot, first, count, to):
        rows = pl.ds(j * CH + first, count)
        src = dn.at[0, rows] if w == 1 and from_slot == 0 else W.at[w, from_slot, rows]
        ag[w, j, k] = send(src, W.at[w, to_slot, rows], ags.at[w, j, k], agr.at[w, j, k], to)

    def ag_own_z(w, j):
        ag_send(w, j, 2, 0, 4, 0, CH, zp)

    def ag_own_y(w, j):
        ag_send(w, j, 0, 0, 3, 0, CH, yp)
        ag_send(w, j, 1, 0, 1, 0, CH, ym)

    def ag_half(w, j):
        ag[w, j, 0].wait_recv()
        ag_send(w, j, 5, 3, 2, 0, HALF, yp)
        if j in BY_Z_AG:
            ag_send(w, j, 8, 3, 7, HALF, HALF, zp)
        ag[w, j, 1].wait_recv()
        ag_send(w, j, 6, 1, 2, HALF, HALF, ym)
        if j in BY_Z_AG:
            ag_send(w, j, 9, 1, 5, HALF, HALF, zp)

    def ag_far(w, j):
        ag[w, j, 2].wait_recv()
        count = HALF if j in BY_Z_AG else CH
        ag_send(w, j, 3, 4, 7, 0, count, yp)
        ag_send(w, j, 4, 4, 5, 0, count, ym)

    def ag_last(w, j):
        ag[w, j, 5].wait_recv()
        ag[w, j, 6].wait_recv()
        ag_send(w, j, 7, 2, 6, 0, CH, zp)

    def ag_end(w, j):
        for k in (3, 4, 7, 8, 9) if j in BY_Z_AG else (3, 4, 7):
            ag[w, j, k].wait_recv()

    def forward(w, j, slots, first):
        rows = pl.ds(j * CH, CH)

        @pl.loop(0, 4)
        def _(t):
            at = pl.ds(pl.multiple_of(t * 128, 128), 128)
            total = None if first else A[w, at]
            for s in slots:
                part = jnp.dot(X[w, s, at, rows], W[w, s, rows], preferred_element_type=jnp.float32)
                total = part if total is None else total + part
            A[w, at] = total

    ag_own_z(1, 0)
    ag_own_y(1, 0)
    for j in range(NCH):
        up_load[j].wait()
        W[0, 0, chunk[j]] = U[chunk[j]].astype(jnp.bfloat16)
        ag_own_z(0, j)
        ag_own_y(0, j)

    x_local, x_send = [[], []], [[], []]
    for w, src in enumerate((tok, cot)):
        for s in range(8):
            mine = pl.ds(pl.multiple_of(shard_at(s % 4, s // 4, c) * ROWS, ROWS), ROWS)
            its = pl.ds(pl.multiple_of(shard_at(s % 4, s // 4, 1 - c) * ROWS, ROWS), ROWS)
            copy = pltpu.make_async_copy(src.at[0, :, mine], X.at[w, s, pl.ds(0, TOK)], x_sem.at[w, s])
            copy.start()
            x_local[w].append(copy)
            x_send[w].append(
                send(src.at[0, :, its], X.at[w, s, pl.ds(TOK, TOK)], xs_sem.at[w, s], xr_sem.at[w, s], partner)
            )
    dn_load.start()

    def x_wait(w):
        for s in range(8):
            x_local[w][s].wait()
            x_send[w][s].wait_recv()

    near, far = (0, 1, 3, 4), (2, 5, 6, 7)
    ag_own_z(1, 1)
    ag_own_z(1, 2)
    ag_half(1, 0)
    ag_far(1, 0)
    ag_half(0, 0)
    ag_far(0, 0)
    ag_own_y(1, 1)
    x_wait(0)
    forward(0, 0, near, True)
    ag_half(0, 1)
    ag_far(0, 1)
    ag_own_y(1, 2)
    ag_last(1, 0)
    ag_last(0, 0)
    forward(0, 1, near, False)
    ag_half(0, 2)
    ag_far(0, 2)
    for copy in late:
        copy.start()
    forward(0, 2, near, False)
    ag_last(0, 1)
    ag_end(0, 0)
    forward(0, 0, far, False)
    ag_half(1, 1)
    ag_far(1, 1)
    ag_last(0, 2)
    ag_end(0, 1)
    forward(0, 1, far, False)
    ag_half(1, 2)
    ag_far(1, 2)
    ag_end(0, 2)
    forward(0, 2, far, False)

    def swap_partial(w):
        return send(A.at[w, pl.ds(TOK, TOK)], R.at[w], ps.at[w], pr.at[w], partner)

    def swap_hidden(w):
        return send(G.at[w, 0], G.at[w, 1], gs.at[w], gr.at[w], partner)

    def terms(w, j):
        rows = pl.ds(j * CH, CH)
        scale = D ** (-0.5) if w == 0 else FFW ** (-0.5)

        @pl.loop(0, 8)
        def _(s):
            part = jnp.dot(G[w, 0], X[w, s, pl.ds(0, TOK), rows], preferred_element_type=jnp.float32)
            part += jnp.dot(G[w, 1], X[w, s, pl.ds(TOK, TOK), rows], preferred_element_type=jnp.float32)
            T[w, j, s] = (part * scale).astype(jnp.bfloat16)

    partial = swap_partial(0)
    x_wait(1)
    dn_load.wait()
    forward(1, 0, near, True)
    ag_last(1, 1)
    partial.wait_recv()

    @pl.loop(0, 2)
    def _(t):
        at = pl.ds(pl.multiple_of(t * 128, 128), 128)
        v = (A[0, at] + R[0, at]) * D ** (-0.5)
        R[0, at] = v
        act = 0.5 * v * (1.0 + jnp.tanh(GELU_K * (v + GELU_C * (v * v * v))))
        G[1, 0, :, at] = act.T.astype(jnp.bfloat16)

    hidden = swap_hidden(1)
    rs = {}

    def rs_send(w, j, k, src, dst, to):
        rs[w, j, k] = send(src, dst, rss.at[w, j, k], rsr.at[w, j, k], to)

    low, high, full = pl.ds(0, HALF_F), pl.ds(HALF_F, HALF_F), pl.ds(0, FFW)

    def rs_one(w, j):
        by_z = j in BY_Z_RS
        to_yp, to_ym = (low, high) if by_z else (full, full)
        rs_send(w, j, 0, T.at[w, j, 6], B.at[w, j, 0], zp)
        rs_send(w, j, 1, T.at[w, j, 5, to_yp], B.at[w, j, 1, to_yp], yp)
        rs_send(w, j, 2, T.at[w, j, 7, to_ym], B.at[w, j, 2, to_ym], ym)
        if by_z:
            rs_send(w, j, 8, T.at[w, j, 5, high], B.at[w, j, 7, high], zp)
            rs_send(w, j, 9, T.at[w, j, 7, low], B.at[w, j, 7, low], zp)

    def add(w, j, slot, rows, *held):
        total = T[w, j, slot, rows].astype(jnp.float32)
        for k in held:
            total += B[w, j, k, rows].astype(jnp.float32)
        T[w, j, slot, rows] = total.astype(jnp.bfloat16)

    def rs_two(w, j):
        rs[w, j, 0].wait_recv()
        add(w, j, 2, full, 0)
        rs_send(w, j, 3, T.at[w, j, 2, low], B.at[w, j, 3, low], yp)
        rs_send(w, j, 4, T.at[w, j, 2, high], B.at[w, j, 3, high], ym)
        rs[w, j, 1].wait_recv()
        rs[w, j, 2].wait_recv()
        if j in BY_Z_RS:
            add(w, j, 4, low, 1)
            add(w, j, 4, high, 2)
        else:
            add(w, j, 4, full, 1, 2)
        rs_send(w, j, 5, T.at[w, j, 4], B.at[w, j, 4], zp)

    def rs_three(w, j):
        by_z = j in BY_Z_RS
        rs[w, j, 3].wait_recv()
        add(w, j, 1, low, 3)
        if by_z:
            rs[w, j, 8].wait_recv()
            add(w, j, 1, high, 7)
        rs_send(w, j, 6, T.at[w, j, 1], B.at[w, j, 5], yp)
        rs[w, j, 4].wait_recv()
        add(w, j, 3, high, 3)
        if by_z:
            rs[w, j, 9].wait_recv()
            add(w, j, 3, low, 7)
        rs_send(w, j, 7, T.at[w, j, 3], B.at[w, j, 6], ym)

    def rs_four(w, j):
        for k in (5, 6, 7):
            rs[w, j, k].wait_recv()
        total = T[w, j, 0].astype(jnp.float32)
        for k in (4, 5, 6):
            total += B[w, j, k].astype(jnp.float32)
        return total.T

    ag_end(1, 0)
    forward(1, 0, far, False)
    forward(1, 1, near, False)
    hidden.wait_recv()
    terms(1, 0)
    ag_last(1, 2)
    rs_one(1, 0)
    forward(1, 2, near, False)
    terms(1, 1)
    rs_one(1, 1)
    terms(1, 2)
    rs_one(1, 2)
    ag_end(1, 1)
    forward(1, 1, far, False)
    ag_end(1, 2)
    forward(1, 2, far, False)
    partial = swap_partial(1)
    partial.wait_recv()

    @pl.loop(0, 2)
    def _(t):
        at = pl.ds(pl.multiple_of(t * 128, 128), 128)
        upstream = (A[1, at] + R[1, at]) * FFW ** (-0.5)
        v = R[0, at]
        squared = v * v
        th = jnp.tanh(GELU_K * (v + GELU_C * (v * squared)))
        slope = 0.5 * (1.0 + th) + 0.5 * v * (1.0 - th * th) * (GELU_K * (1.0 + 3.0 * GELU_C * squared))
        G[0, 0, :, at] = (upstream * slope).T.astype(jnp.bfloat16)

    hidden = swap_hidden(0)
    hidden.wait_recv()
    for j in range(NCH):
        terms(0, j)
        rs_one(0, j)
        rs_two(1, j)
    for j in range(NCH):
        rs_two(0, j)
    for copy in late:
        copy.wait()

    ar = {}

    def adam(j):
        rows = pl.ds(j * CH, CH)
        grad = rs_four(0, j)
        first = beta_one * o_m1[rows] + (1.0 - beta_one) * grad
        o_m1[rows] = first
        second = beta_two * o_m2[rows] + (1.0 - beta_two) * grad * grad
        o_m2[rows] = second
        master = U[rows]
        stepped = master - inner_rate * (
            first / fix_one / (jnp.sqrt(second / fix_two) + adam_eps) + decay_rate * master
        )
        PS[j] = (o_anc[rows] - stepped).astype(jnp.bfloat16)
        for p in range(1, N_REP):
            piece = pl.ds(pl.multiple_of(peers[p][0] * PIECE, PIECE), PIECE)
            back = (p // 4) * 4 + (-p) % 4
            ar[j, p] = send(PS.at[j, piece], PR.at[j, back], ars.at[j, p - 1], arr.at[j, back - 1], peers[p])

    mean = {}

    def reduce_mean(j):
        mine = pl.ds(pl.multiple_of(rep * PIECE, PIECE), PIECE)
        total = PS[j, mine].astype(jnp.float32)
        for p in range(1, N_REP):
            ar[j, p].wait_recv()
        for p in range(1, N_REP):
            total += PR[j, p].astype(jnp.float32)
        MN[j, mine] = (total / N_REP).astype(jnp.bfloat16)
        for p in range(1, N_REP):
            back = (p // 4) * 4 + (-p) % 4
            mean[j, p] = send(MN.at[j, mine], MN.at[j, mine], mns.at[j, p - 1], mnr.at[j, back - 1], peers[p])

    def outer(j):
        rows = pl.ds(j * CH, CH)
        for p in range(1, N_REP):
            mean[j, p].wait_recv()
        outer_mean = MN[j].astype(jnp.float32)
        new_momentum = outer_mu * o_mom[rows] + outer_mean
        o_mom[rows] = new_momentum
        o_anc[rows] = o_anc[rows] - outer_rate * (outer_mean + outer_mu * new_momentum)

    def down(j):
        rows = pl.ds(j * CH, CH)
        o_acc[rows] = o_acc[rows] + rs_four(1, j)

    for j in range(NCH):
        rs_three(0, j)
    rs_three(1, 0)
    adam(0)
    rs_three(1, 1)
    adam(1)
    rs_three(1, 2)
    adam(2)
    for j in range(NCH):
        reduce_mean(j)
    down(0)
    down(1)
    for j in range(NCH):
        outer(j)
    down(2)
    for copy in sends:
        copy.wait_send()


def place(anc, mom, m1, m2, acc, o_anc, o_mom, o_m1, o_m2, o_acc, sem):
    pairs = ((anc, o_anc), (mom, o_mom), (m1, o_m1.at[0]), (m2, o_m2.at[0]), (acc, o_acc.at[0]))
    copies = [pltpu.make_async_copy(src, dst, sem.at[i]) for i, (src, dst) in enumerate(pairs)]
    for copy in copies:
        copy.start()
    for copy in copies:
        copy.wait()


def on_device(tokens, cotangent, inner_up, adam_first, adam_second, inner_down, down_accum, anchor_up, outer_momentum):
    flat = jax.ShapeDtypeStruct((ROWS, FFW), jnp.float32)
    deep = jax.ShapeDtypeStruct((1, ROWS, FFW), jnp.float32)
    dma = pltpu.SemaphoreType.DMA
    bf16, f32 = jnp.bfloat16, jnp.float32
    held = pl.pallas_call(
        kernel,
        out_shape=(pltpu.VMEM((ROWS, FFW), f32),) * 5,
        in_specs=[pl.BlockSpec(memory_space=pl.ANY)] * 9,
        out_specs=[pl.BlockSpec(memory_space=pltpu.VMEM)] * 5,
        scratch_shapes=[
            pltpu.VMEM((2, 8, 2 * TOK, ROWS), bf16),
            pltpu.VMEM((2, 8, ROWS, FFW), bf16),
            pltpu.VMEM((2, 2 * TOK, FFW), f32),
            pltpu.VMEM((2, TOK, FFW), f32),
            pltpu.VMEM((2, 2, FFW, TOK), bf16),
            pltpu.VMEM((2, NCH, 8, FFW, CH), bf16),
            pltpu.VMEM((2, NCH, 8, FFW, CH), bf16),
            pltpu.VMEM((ROWS, FFW), f32),
            pltpu.VMEM((NCH, CH, FFW), bf16),
            pltpu.VMEM((NCH, N_REP, PIECE, FFW), bf16),
            pltpu.VMEM((NCH, CH, FFW), bf16),
            dma((9,)),
            dma((2, 8)),
            dma((2, 8)),
            dma((2, 8)),
            dma((2, NCH, 10)),
            dma((2, NCH, 10)),
            dma((2, NCH, 10)),
            dma((2, NCH, 10)),
            dma((2,)),
            dma((2,)),
            dma((2,)),
            dma((2,)),
            dma((NCH, N_REP - 1)),
            dma((NCH, N_REP - 1)),
            dma((NCH, N_REP - 1)),
            dma((NCH, N_REP - 1)),
        ],
        name="window",
        compiler_params=pltpu.CompilerParams(
            collective_id=0, has_side_effects=True, vmem_limit_bytes=52 * 2**20
        ),
        cost_estimate=pl.CostEstimate(flops=9_700_000_000, bytes_accessed=30_000_000, transcendentals=200_000),
    )(tokens, cotangent, inner_up, adam_first, adam_second, inner_down, down_accum, anchor_up, outer_momentum)
    return pl.pallas_call(
        place,
        out_shape=(flat, flat, deep, deep, deep),
        in_specs=[pl.BlockSpec(memory_space=pltpu.VMEM)] * 5,
        out_specs=[pl.BlockSpec(memory_space=pl.ANY)] * 5,
        scratch_shapes=[dma((5,))],
        name="place",
        compiler_params=pltpu.CompilerParams(vmem_limit_bytes=2**20),
    )(*(pltpu.with_memory_space_constraint(value, pltpu.VMEM) for value in held))


def solution(mesh):
    return jax.shard_map(
        on_device,
        mesh=mesh,
        in_specs=(
            P("replica", "shard", None),
            P("replica", "shard", None),
            P("replica", "shard", None),
            P("replica", "shard", None),
            P("replica", "shard", None),
            P("replica", "shard", None),
            P("replica", "shard", None),
            P("shard", None),
            P("shard", None),
        ),
        out_specs=(
            P("shard", None),
            P("shard", None),
            P("replica", "shard", None),
            P("replica", "shard", None),
            P("replica", "shard", None),
        ),
        check_vma=False,
    )
```

time: 160 us -> 146 us (0.912)
  local copies, waits for them, and re-layouts: 8.56 us -> 0 us
  Pallas kernels: 151 us -> 145 us
    unnamed x13 -> x0, local copies, waits for them, and re-layouts: 8.56 us -> none
    pallas_call x1 -> x2, Pallas kernels: 151 us -> 145 us  [the longest x1 142 us: on_device(): pl.pallas_call(kernel, out_shape=(pltpu.VMEM((ROWS, FFW), f32),) * 5, in_...]
where the time goes in v2:
time: 146 us
  Pallas kernels  145 us (99%)
    pallas_call x1, Pallas kernels, on_device(): pl.pallas_call(kernel, out_shape=(pltpu.VMEM((ROWS, FFW), f32),) * 5, in_...  142 us

profile of v2, /device:TPU:0, one launch (start us, length us, event | category | flops | bytes accessed | tf_op | source)
XLA Modules:
  0.0 145.7 jit_solution(1806546750904986861)
XLA Ops:
  0.6 142.4 %window.1 = (f32[768,384]{1,0:T(8,128)S(1)}, f32[768,384]{1,0:T(8,128)S(1)}, f32[768,384]{1,0:T(8,128)S(1)}, f32[768,384]{1,0:T(8,128)S(1)}, f32[768,384]{1,0:T(8,128)S(1)}) custom-call(bf16[1,256,12288]{2,1,0:T(8,128)(2,1)} %tok.1, bf16[1,256,12288]{2,1,0:T(8,128)(2,1)} %cot.1, f32[1,768,384]{2,1,0:T(8,128)} %up.1, f32[1,768,384]{2,1,0:T(8,128)} %m1.1, ...), custom_call_target="tpu_custom_call" | custom-call | flops 9699999744 | bytes 30000000 | tf_op jit(solution)/shard_map/window/pallas_call | solution.py:408
  143.1 2.6 %place.1 = (f32[768,384]{1,0:T(8,128)}, f32[768,384]{1,0:T(8,128)}, f32[1,768,384]{2,1,0:T(8,128)}, f32[1,768,384]{2,1,0:T(8,128)}, f32[1,768,384]{2,1,0:T(8,128)}) custom-call(f32[768,384]{1,0:T(8,128)S(1)} %get-tuple-element.10.anc, f32[768,384]{1,0:T(8,128)S(1)} %get-tuple-element.11.mom, f32[768,384]{1,0:T(8,128)S(1)} %get-tuple-element.12.m1, ...), custom_call_target="tpu_custom_call" | custom-call | tf_op jit(solution)/shard_map/place/pallas_call | solution.py:448

commit v3 on v2

--- a/solution.py
+++ b/solution.py
@@ -15,9 +15,10 @@
 HALF = CH // 2
 HALF_F = FFW // 2
 N_REP = 8
-PIECE = CH // N_REP
-BY_Z_AG = (0,)
-BY_Z_RS = ()
+N_X = 4
+PIECE = CH // N_X
+BY_Z_AG = ((0, 1), (0, 2))
+BY_Z_RS = ((0, 0),)
 
 beta_one = 0.8
 beta_two = 0.95
@@ -52,13 +53,11 @@
     ym = (rep, shard_at(3, 0, c))
     zp = (rep, shard_at(0, 1, c))
 
-    def peer(p):
-        return ((zl + p // 4) % 2) * 4 + (x + p % 4) % 4
-
-    peers = [(peer(p), shd) for p in range(N_REP)]
+    beside = [(zl * 4 + (x + p) % 4, shd) for p in range(4)]
+    above = ((1 - zl) * 4 + x, shd)
 
     barrier = pltpu.get_barrier_semaphore()
-    others = [partner, yp, ym, zp] + peers[1:]
+    others = [partner, yp, ym, zp, above] + beside[1:]
     for other in others:
         pl.semaphore_signal(barrier, inc=1, device_id=other, device_id_type=MESH)
 
@@ -100,16 +99,16 @@
     def ag_half(w, j):
         ag[w, j, 0].wait_recv()
         ag_send(w, j, 5, 3, 2, 0, HALF, yp)
-        if j in BY_Z_AG:
+        if (w, j) in BY_Z_AG:
             ag_send(w, j, 8, 3, 7, HALF, HALF, zp)
         ag[w, j, 1].wait_recv()
         ag_send(w, j, 6, 1, 2, HALF, HALF, ym)
-        if j in BY_Z_AG:
+        if (w, j) in BY_Z_AG:
             ag_send(w, j, 9, 1, 5, HALF, HALF, zp)
 
     def ag_far(w, j):
         ag[w, j, 2].wait_recv()
-        count = HALF if j in BY_Z_AG else CH
+        count = HALF if (w, j) in BY_Z_AG else CH
         ag_send(w, j, 3, 4, 7, 0, count, yp)
         ag_send(w, j, 4, 4, 5, 0, count, ym)
 
@@ -119,10 +118,14 @@
         ag_send(w, j, 7, 2, 6, 0, CH, zp)
 
     def ag_end(w, j):
-        for k in (3, 4, 7, 8, 9) if j in BY_Z_AG else (3, 4, 7):
+        for k in (3, 4, 7, 8, 9) if (w, j) in BY_Z_AG else (3, 4, 7):
             ag[w, j, k].wait_recv()
 
-    def forward(w, j, slots, first):
+    begun = set()
+
+    def forward(w, j, slots):
+        first = w not in begun
+        begun.add(w)
         rows = pl.ds(j * CH, CH)
 
         @pl.loop(0, 4)
@@ -134,71 +137,62 @@
                 total = part if total is None else total + part
             A[w, at] = total
 
-    ag_own_z(1, 0)
-    ag_own_y(1, 0)
-    for j in range(NCH):
+    def up_cast(j):
         up_load[j].wait()
         W[0, 0, chunk[j]] = U[chunk[j]].astype(jnp.bfloat16)
-        ag_own_z(0, j)
-        ag_own_y(0, j)
 
     x_local, x_send = [[], []], [[], []]
-    for w, src in enumerate((tok, cot)):
-        for s in range(8):
-            mine = pl.ds(pl.multiple_of(shard_at(s % 4, s // 4, c) * ROWS, ROWS), ROWS)
-            its = pl.ds(pl.multiple_of(shard_at(s % 4, s // 4, 1 - c) * ROWS, ROWS), ROWS)
-            copy = pltpu.make_async_copy(src.at[0, :, mine], X.at[w, s, pl.ds(0, TOK)], x_sem.at[w, s])
+
+    def x_start():
+        for w, src in enumerate((tok, cot)):
+            for s in range(8):
+                mine = pl.ds(pl.multiple_of(shard_at(s % 4, s // 4, c) * ROWS, ROWS), ROWS)
+                its = pl.ds(pl.multiple_of(shard_at(s % 4, s // 4, 1 - c) * ROWS, ROWS), ROWS)
+                copy = pltpu.make_async_copy(src.at[0, :, mine], X.at[w, s, pl.ds(0, TOK)], x_sem.at[w, s])
+                copy.start()
+                x_local[w].append(copy)
+                x_send[w].append(
+                    send(src.at[0, :, its], X.at[w, s, pl.ds(TOK, TOK)], xs_sem.at[w, s], xr_sem.at[w, s], partner)
+                )
+        dn_load.start()
+        for copy in late:
             copy.start()
-            x_local[w].append(copy)
-            x_send[w].append(
-                send(src.at[0, :, its], X.at[w, s, pl.ds(TOK, TOK)], xs_sem.at[w, s], xr_sem.at[w, s], partner)
-            )
-    dn_load.start()
 
     def x_wait(w):
         for s in range(8):
             x_local[w][s].wait()
             x_send[w][s].wait_recv()
+        if w == 1:
+            dn_load.wait()
 
     near, far = (0, 1, 3, 4), (2, 5, 6, 7)
-    ag_own_z(1, 1)
-    ag_own_z(1, 2)
-    ag_half(1, 0)
-    ag_far(1, 0)
-    ag_half(0, 0)
-    ag_far(0, 0)
-    ag_own_y(1, 1)
-    x_wait(0)
-    forward(0, 0, near, True)
-    ag_half(0, 1)
-    ag_far(0, 1)
-    ag_own_y(1, 2)
-    ag_last(1, 0)
-    ag_last(0, 0)
-    forward(0, 1, near, False)
-    ag_half(0, 2)
-    ag_far(0, 2)
-    for copy in late:
-        copy.start()
-    forward(0, 2, near, False)
-    ag_last(0, 1)
-    ag_end(0, 0)
-    forward(0, 0, far, False)
-    ag_half(1, 1)
-    ag_far(1, 1)
-    ag_last(0, 2)
-    ag_end(0, 1)
-    forward(0, 1, far, False)
-    ag_half(1, 2)
-    ag_far(1, 2)
-    ag_end(0, 2)
-    forward(0, 2, far, False)
+    partial, hidden = {}, {}
+
+    def act():
+        @pl.loop(0, 2)
+        def _(t):
+            at = pl.ds(pl.multiple_of(t * 128, 128), 128)
+            v = (A[0, at] + R[0, at]) * D ** (-0.5)
+            R[0, at] = v
+            act = 0.5 * v * (1.0 + jnp.tanh(GELU_K * (v + GELU_C * (v * v * v))))
+            G[1, 0, :, at] = act.T.astype(jnp.bfloat16)
+
+    def grad():
+        @pl.loop(0, 2)
+        def _(t):
+            at = pl.ds(pl.multiple_of(t * 128, 128), 128)
+            upstream = (A[1, at] + R[1, at]) * FFW ** (-0.5)
+            v = R[0, at]
+            squared = v * v
+            th = jnp.tanh(GELU_K * (v + GELU_C * (v * squared)))
+            slope = 0.5 * (1.0 + th) + 0.5 * v * (1.0 - th * th) * (GELU_K * (1.0 + 3.0 * GELU_C * squared))
+            G[0, 0, :, at] = (upstream * slope).T.astype(jnp.bfloat16)
 
     def swap_partial(w):
-        return send(A.at[w, pl.ds(TOK, TOK)], R.at[w], ps.at[w], pr.at[w], partner)
+        partial[w] = send(A.at[w, pl.ds(TOK, TOK)], R.at[w], ps.at[w], pr.at[w], partner)
 
     def swap_hidden(w):
-        return send(G.at[w, 0], G.at[w, 1], gs.at[w], gr.at[w], partner)
+        hidden[w] = send(G.at[w, 0], G.at[w, 1], gs.at[w], gr.at[w], partner)
 
     def terms(w, j):
         rows = pl.ds(j * CH, CH)
@@ -210,22 +204,6 @@
             part += jnp.dot(G[w, 1], X[w, s, pl.ds(TOK, TOK), rows], preferred_element_type=jnp.float32)
             T[w, j, s] = (part * scale).astype(jnp.bfloat16)
 
-    partial = swap_partial(0)
-    x_wait(1)
-    dn_load.wait()
-    forward(1, 0, near, True)
-    ag_last(1, 1)
-    partial.wait_recv()
-
-    @pl.loop(0, 2)
-    def _(t):
-        at = pl.ds(pl.multiple_of(t * 128, 128), 128)
-        v = (A[0, at] + R[0, at]) * D ** (-0.5)
-        R[0, at] = v
-        act = 0.5 * v * (1.0 + jnp.tanh(GELU_K * (v + GELU_C * (v * v * v))))
-        G[1, 0, :, at] = act.T.astype(jnp.bfloat16)
-
-    hidden = swap_hidden(1)
     rs = {}
 
     def rs_send(w, j, k, src, dst, to):
@@ -233,10 +211,12 @@
 
     low, high, full = pl.ds(0, HALF_F), pl.ds(HALF_F, HALF_F), pl.ds(0, FFW)
 
-    def rs_one(w, j):
-        by_z = j in BY_Z_RS
+    def rs_one_z(w, j):
+        rs_send(w, j, 0, T.at[w, j, 6], B.at[w, j, 0], zp)
+
+    def rs_one_y(w, j):
+        by_z = (w, j) in BY_Z_RS
         to_yp, to_ym = (low, high) if by_z else (full, full)
-        rs_send(w, j, 0, T.at[w, j, 6], B.at[w, j, 0], zp)
         rs_send(w, j, 1, T.at[w, j, 5, to_yp], B.at[w, j, 1, to_yp], yp)
         rs_send(w, j, 2, T.at[w, j, 7, to_ym], B.at[w, j, 2, to_ym], ym)
         if by_z:
@@ -249,82 +229,46 @@
             total += B[w, j, k, rows].astype(jnp.float32)
         T[w, j, slot, rows] = total.astype(jnp.bfloat16)
 
-    def rs_two(w, j):
+    def rs_two_y(w, j):
         rs[w, j, 0].wait_recv()
         add(w, j, 2, full, 0)
         rs_send(w, j, 3, T.at[w, j, 2, low], B.at[w, j, 3, low], yp)
         rs_send(w, j, 4, T.at[w, j, 2, high], B.at[w, j, 3, high], ym)
+
+    def rs_two_z(w, j):
         rs[w, j, 1].wait_recv()
         rs[w, j, 2].wait_recv()
-        if j in BY_Z_RS:
+        if (w, j) in BY_Z_RS:
             add(w, j, 4, low, 1)
             add(w, j, 4, high, 2)
         else:
             add(w, j, 4, full, 1, 2)
         rs_send(w, j, 5, T.at[w, j, 4], B.at[w, j, 4], zp)
 
-    def rs_three(w, j):
-        by_z = j in BY_Z_RS
+    def rs_three_a(w, j):
+        if (w, j) in BY_Z_RS:
+            rs[w, j, 8].wait_recv()
+            add(w, j, 1, high, 7)
+            rs[w, j, 9].wait_recv()
+            add(w, j, 3, low, 7)
+        rs_send(w, j, 10, T.at[w, j, 1, high], B.at[w, j, 5, high], yp)
+        rs_send(w, j, 11, T.at[w, j, 3, low], B.at[w, j, 6, low], ym)
+
+    def rs_three_b(w, j):
         rs[w, j, 3].wait_recv()
         add(w, j, 1, low, 3)
-        if by_z:
-            rs[w, j, 8].wait_recv()
-            add(w, j, 1, high, 7)
-        rs_send(w, j, 6, T.at[w, j, 1], B.at[w, j, 5], yp)
+        rs_send(w, j, 6, T.at[w, j, 1, low], B.at[w, j, 5, low], yp)
         rs[w, j, 4].wait_recv()
         add(w, j, 3, high, 3)
-        if by_z:
-            rs[w, j, 9].wait_recv()
-            add(w, j, 3, low, 7)
-        rs_send(w, j, 7, T.at[w, j, 3], B.at[w, j, 6], ym)
+        rs_send(w, j, 7, T.at[w, j, 3, high], B.at[w, j, 6, high], ym)
 
     def rs_four(w, j):
-        for k in (5, 6, 7):
+        for k in (5, 6, 7, 10, 11):
             rs[w, j, k].wait_recv()
         total = T[w, j, 0].astype(jnp.float32)
         for k in (4, 5, 6):
             total += B[w, j, k].astype(jnp.float32)
         return total.T
-
-    ag_end(1, 0)
-    forward(1, 0, far, False)
-    forward(1, 1, near, False)
-    hidden.wait_recv()
-    terms(1, 0)
-    ag_last(1, 2)
-    rs_one(1, 0)
-    forward(1, 2, near, False)
-    terms(1, 1)
-    rs_one(1, 1)
-    terms(1, 2)
-    rs_one(1, 2)
-    ag_end(1, 1)
-    forward(1, 1, far, False)
-    ag_end(1, 2)
-    forward(1, 2, far, False)
-    partial = swap_partial(1)
-    partial.wait_recv()
-
-    @pl.loop(0, 2)
-    def _(t):
-        at = pl.ds(pl.multiple_of(t * 128, 128), 128)
-        upstream = (A[1, at] + R[1, at]) * FFW ** (-0.5)
-        v = R[0, at]
-        squared = v * v
-        th = jnp.tanh(GELU_K * (v + GELU_C * (v * squared)))
-        slope = 0.5 * (1.0 + th) + 0.5 * v * (1.0 - th * th) * (GELU_K * (1.0 + 3.0 * GELU_C * squared))
-        G[0, 0, :, at] = (upstream * slope).T.astype(jnp.bfloat16)
-
-    hidden = swap_hidden(0)
-    hidden.wait_recv()
-    for j in range(NCH):
-        terms(0, j)
-        rs_one(0, j)
-        rs_two(1, j)
-    for j in range(NCH):
-        rs_two(0, j)
-    for copy in late:
-        copy.wait()
 
     ar = {}
 
@@ -340,28 +284,32 @@
             first / fix_one / (jnp.sqrt(second / fix_two) + adam_eps) + decay_rate * master
         )
         PS[j] = (o_anc[rows] - stepped).astype(jnp.bfloat16)
-        for p in range(1, N_REP):
-            piece = pl.ds(pl.multiple_of(peers[p][0] * PIECE, PIECE), PIECE)
-            back = (p // 4) * 4 + (-p) % 4
-            ar[j, p] = send(PS.at[j, piece], PR.at[j, back], ars.at[j, p - 1], arr.at[j, back - 1], peers[p])
+        for p in range(1, N_X):
+            piece = pl.ds(pl.multiple_of(((x + p) % N_X) * PIECE, PIECE), PIECE)
+            ar[j, p] = send(PS.at[j, piece], PR.at[j, N_X - p], ars.at[j, p], arr.at[j, N_X - p], beside[p])
 
     mean = {}
 
-    def reduce_mean(j):
-        mine = pl.ds(pl.multiple_of(rep * PIECE, PIECE), PIECE)
-        total = PS[j, mine].astype(jnp.float32)
-        for p in range(1, N_REP):
+    def sum_x(j):
+        for p in range(1, N_X):
             ar[j, p].wait_recv()
-        for p in range(1, N_REP):
+        total = PS[j, pl.ds(pl.multiple_of(x * PIECE, PIECE), PIECE)].astype(jnp.float32)
+        for p in range(1, N_X):
             total += PR[j, p].astype(jnp.float32)
+        PR[j, 0] = total.astype(jnp.bfloat16)
+        ar[j, 0] = send(PR.at[j, 0], PR.at[j, N_X], ars.at[j, 0], arr.at[j, 0], above)
+
+    def sum_z(j):
+        ar[j, 0].wait_recv()
+        mine = pl.ds(pl.multiple_of(x * PIECE, PIECE), PIECE)
+        total = PR[j, 0].astype(jnp.float32) + PR[j, N_X].astype(jnp.float32)
         MN[j, mine] = (total / N_REP).astype(jnp.bfloat16)
-        for p in range(1, N_REP):
-            back = (p // 4) * 4 + (-p) % 4
-            mean[j, p] = send(MN.at[j, mine], MN.at[j, mine], mns.at[j, p - 1], mnr.at[j, back - 1], peers[p])
+        for p in range(1, N_X):
+            mean[j, p] = send(MN.at[j, mine], MN.at[j, mine], mns.at[j, p], mnr.at[j, N_X - p], beside[p])
 
     def outer(j):
         rows = pl.ds(j * CH, CH)
-        for p in range(1, N_REP):
+        for p in range(1, N_X):
             mean[j, p].wait_recv()
         outer_mean = MN[j].astype(jnp.float32)
         new_momentum = outer_mu * o_mom[rows] + outer_mean
@@ -372,21 +320,129 @@
         rows = pl.ds(j * CH, CH)
         o_acc[rows] = o_acc[rows] + rs_four(1, j)
 
-    for j in range(NCH):
-        rs_three(0, j)
-    rs_three(1, 0)
+    ag_own_z(1, 2)
+    ag_own_y(1, 1)
+    up_cast(2)
+    up_cast(1)
+    up_cast(0)
+    ag_own_y(0, 0)
+    ag_own_z(0, 2)
+    ag_own_z(0, 1)
+    ag_own_y(0, 1)
+    x_start()
+    ag_own_z(0, 0)
+    ag_own_y(0, 2)
+    ag_own_y(1, 0)
+    ag_far(0, 1)
+    ag_half(0, 0)
+    x_wait(0)
+    ag_half(0, 1)
+    ag_own_y(1, 2)
+    ag_half(0, 2)
+    ag_half(1, 0)
+    ag_own_z(1, 0)
+    forward(0, 1, near)
+    ag_far(0, 0)
+    ag_last(0, 0)
+    ag_last(0, 1)
+    ag_last(0, 2)
+    ag_own_z(1, 1)
+    ag_far(0, 2)
+    ag_half(1, 1)
+    ag_last(1, 0)
+    forward(0, 0, near)
+    ag_end(0, 1)
+    forward(0, 1, far)
+    ag_far(1, 0)
+    forward(0, 2, near)
+    ag_end(0, 0)
+    forward(0, 0, far)
+    ag_end(0, 2)
+    ag_half(1, 2)
+    forward(0, 2, far)
+    x_wait(1)
+    swap_partial(0)
+    ag_last(1, 1)
+    forward(1, 0, near)
+    partial[0].wait_recv()
+    act()
+    swap_hidden(1)
+    ag_far(1, 1)
+    forward(1, 1, near)
+    hidden[1].wait_recv()
+    terms(1, 1)
+    ag_last(1, 2)
+    ag_far(1, 2)
+    ag_end(1, 0)
+    forward(1, 2, near)
+    rs_one_z(1, 1)
+    terms(1, 0)
+    ag_end(1, 1)
+    rs_one_z(1, 0)
+    rs_three_a(1, 1)
+    rs_one_y(1, 0)
+    forward(1, 1, far)
+    forward(1, 0, far)
+    ag_end(1, 2)
+    forward(1, 2, far)
+    swap_partial(1)
+    rs_one_y(1, 1)
+    partial[1].wait_recv()
+    grad()
+    swap_hidden(0)
+    hidden[0].wait_recv()
+    terms(0, 2)
+    rs_one_y(0, 2)
+    rs_three_a(0, 2)
+    rs_one_z(0, 2)
+    terms(0, 1)
+    rs_one_z(0, 1)
+    terms(0, 0)
+    rs_one_y(0, 1)
+    rs_one_z(0, 0)
+    rs_two_y(0, 2)
+    rs_one_y(0, 0)
+    rs_two_z(0, 2)
+    rs_two_y(0, 1)
+    rs_two_y(0, 0)
+    rs_three_b(0, 2)
+    terms(1, 2)
+    rs_three_b(0, 1)
+    rs_three_a(0, 1)
+    rs_two_z(0, 1)
+    rs_three_a(0, 0)
+    rs_two_z(0, 0)
+    rs_one_z(1, 2)
+    rs_three_b(0, 0)
+    rs_two_y(1, 1)
+    rs_two_z(1, 1)
+    rs_one_y(1, 2)
+    rs_two_y(1, 0)
+    rs_three_a(1, 0)
+    for copy in late:
+        copy.wait()
+    adam(2)
+    adam(1)
     adam(0)
-    rs_three(1, 1)
-    adam(1)
-    rs_three(1, 2)
-    adam(2)
-    for j in range(NCH):
-        reduce_mean(j)
+    rs_two_z(1, 0)
+    sum_x(2)
+    sum_x(1)
+    rs_two_y(1, 2)
+    rs_two_z(1, 2)
+    rs_three_b(1, 1)
+    rs_three_b(1, 0)
+    sum_x(0)
+    sum_z(2)
+    rs_three_b(1, 2)
+    sum_z(1)
+    rs_three_a(1, 2)
+    down(1)
+    sum_z(0)
     down(0)
-    down(1)
-    for j in range(NCH):
-        outer(j)
+    outer(2)
+    outer(1)
     down(2)
+    outer(0)
     for copy in sends:
         copy.wait_send()
 
@@ -420,7 +476,7 @@
             pltpu.VMEM((2, NCH, 8, FFW, CH), bf16),
             pltpu.VMEM((ROWS, FFW), f32),
             pltpu.VMEM((NCH, CH, FFW), bf16),
-            pltpu.VMEM((NCH, N_REP, PIECE, FFW), bf16),
+            pltpu.VMEM((NCH, N_X + 1, PIECE, FFW), bf16),
             pltpu.VMEM((NCH, CH, FFW), bf16),
             dma((9,)),
             dma((2, 8)),
@@ -428,16 +484,16 @@
             dma((2, 8)),
             dma((2, NCH, 10)),
             dma((2, NCH, 10)),
-            dma((2, NCH, 10)),
-            dma((2, NCH, 10)),
+            dma((2, NCH, 12)),
+            dma((2, NCH, 12)),
             dma((2,)),
             dma((2,)),
             dma((2,)),
             dma((2,)),
-            dma((NCH, N_REP - 1)),
-            dma((NCH, N_REP - 1)),
-            dma((NCH, N_REP - 1)),
-            dma((NCH, N_REP - 1)),
+            dma((NCH, N_X)),
+            dma((NCH, N_X)),
+            dma((NCH, N_X)),
+            dma((NCH, N_X)),
         ],
         name="window",
         compiler_params=pltpu.CompilerParams(

time: 146 us -> 137 us (0.938)
  Pallas kernels: 145 us -> 137 us
    pallas_call x1, Pallas kernels: 142 us -> 134 us  [on_device(): pl.pallas_call(kernel, out_shape=(pltpu.VMEM((ROWS, FFW), f32),) * 5, in_...]
where the time goes in v3:
time: 137 us
  Pallas kernels  137 us (100%)
    pallas_call x1, Pallas kernels, on_device(): pl.pallas_call(kernel, out_shape=(pltpu.VMEM((ROWS, FFW), f32),) * 5, in_...  134 us

profile of v3, /device:TPU:0, one launch (start us, length us, event | category | flops | bytes accessed | tf_op | source)
XLA Modules:
  0.0 137.4 jit_solution(16893230680857720194)
XLA Ops:
  0.6 134.1 %window.1 = (f32[768,384]{1,0:T(8,128)S(1)}, f32[768,384]{1,0:T(8,128)S(1)}, f32[768,384]{1,0:T(8,128)S(1)}, f32[768,384]{1,0:T(8,128)S(1)}, f32[768,384]{1,0:T(8,128)S(1)}) custom-call(bf16[1,256,12288]{2,1,0:T(8,128)(2,1)} %tok.1, bf16[1,256,12288]{2,1,0:T(8,128)(2,1)} %cot.1, f32[1,768,384]{2,1,0:T(8,128)} %up.1, f32[1,768,384]{2,1,0:T(8,128)} %m1.1, ...), custom_call_target="tpu_custom_call" | custom-call | flops 9699999744 | bytes 30000000 | tf_op jit(solution)/shard_map/window/pallas_call | solution.py:464
  134.8 2.6 %place.1 = (f32[768,384]{1,0:T(8,128)}, f32[768,384]{1,0:T(8,128)}, f32[1,768,384]{2,1,0:T(8,128)}, f32[1,768,384]{2,1,0:T(8,128)}, f32[1,768,384]{2,1,0:T(8,128)}) custom-call(f32[768,384]{1,0:T(8,128)S(1)} %get-tuple-element.10.anc, f32[768,384]{1,0:T(8,128)S(1)} %get-tuple-element.11.mom, f32[768,384]{1,0:T(8,128)S(1)} %get-tuple-element.12.m1, ...), custom_call_target="tpu_custom_call" | custom-call | tf_op jit(solution)/shard_map/place/pallas_call | solution.py:504

commit v4 on v3

--- a/solution.py
+++ b/solution.py
@@ -12,13 +12,14 @@
 ROWS = 768
 CH = 256
 NCH = 3
+LAST = 2
 HALF = CH // 2
 HALF_F = FFW // 2
 N_REP = 8
 N_X = 4
 PIECE = CH // N_X
-BY_Z_AG = ((0, 1), (0, 2))
-BY_Z_RS = ((0, 0),)
+AG_Z = {(0, 1): 128, (0, 2): 128}
+RS_Z = {(0, 0): 192}
 
 beta_one = 0.8
 beta_two = 0.95
@@ -36,7 +37,7 @@
 
 def kernel(
     tok, cot, up, m1, m2, dn, acc, anc, mom,
-    o_anc, o_mom, o_m1, o_m2, o_acc,
+    o_anc, o_mom, o_m1, o_m2, o_acc, E,
     X, W, A, R, G, T, B, U, PS, PR, MN,
     load_sem, x_sem, xs_sem, xr_sem, ags, agr, rss, rsr, ps, pr, gs, gr, ars, arr, mns, mnr,
 ):
@@ -97,18 +98,19 @@
         ag_send(w, j, 1, 0, 1, 0, CH, ym)
 
     def ag_half(w, j):
+        by_z = AG_Z.get((w, j), 0)
         ag[w, j, 0].wait_recv()
         ag_send(w, j, 5, 3, 2, 0, HALF, yp)
-        if (w, j) in BY_Z_AG:
-            ag_send(w, j, 8, 3, 7, HALF, HALF, zp)
+        if by_z:
+            ag_send(w, j, 8, 3, 7, CH - by_z, by_z, zp)
         ag[w, j, 1].wait_recv()
         ag_send(w, j, 6, 1, 2, HALF, HALF, ym)
-        if (w, j) in BY_Z_AG:
-            ag_send(w, j, 9, 1, 5, HALF, HALF, zp)
+        if by_z:
+            ag_send(w, j, 9, 1, 5, CH - by_z, by_z, zp)
 
     def ag_far(w, j):
         ag[w, j, 2].wait_recv()
-        count = HALF if (w, j) in BY_Z_AG else CH
+        count = CH - AG_Z.get((w, j), 0)
         ag_send(w, j, 3, 4, 7, 0, count, yp)
         ag_send(w, j, 4, 4, 5, 0, count, ym)
 
@@ -118,7 +120,7 @@
         ag_send(w, j, 7, 2, 6, 0, CH, zp)
 
     def ag_end(w, j):
-        for k in (3, 4, 7, 8, 9) if (w, j) in BY_Z_AG else (3, 4, 7):
+        for k in (3, 4, 7, 8, 9) if AG_Z.get((w, j)) else (3, 4, 7):
             ag[w, j, k].wait_recv()
 
     begun = set()
@@ -204,6 +206,9 @@
             part += jnp.dot(G[w, 1], X[w, s, pl.ds(TOK, TOK), rows], preferred_element_type=jnp.float32)
             T[w, j, s] = (part * scale).astype(jnp.bfloat16)
 
+        if (w, j) == (1, LAST):
+            E[3] = T[w, j, 0]
+
     rs = {}
 
     def rs_send(w, j, k, src, dst, to):
@@ -211,17 +216,21 @@
 
     low, high, full = pl.ds(0, HALF_F), pl.ds(HALF_F, HALF_F), pl.ds(0, FFW)
 
+    def home(w, j, k):
+        return E.at[k - 4] if (w, j) == (1, LAST) else B.at[w, j, k]
+
     def rs_one_z(w, j):
         rs_send(w, j, 0, T.at[w, j, 6], B.at[w, j, 0], zp)
 
     def rs_one_y(w, j):
-        by_z = (w, j) in BY_Z_RS
-        to_yp, to_ym = (low, high) if by_z else (full, full)
+        by_z = RS_Z.get((w, j), 0)
+        to_yp, to_ym = pl.ds(0, FFW - by_z), pl.ds(by_z, FFW - by_z)
         rs_send(w, j, 1, T.at[w, j, 5, to_yp], B.at[w, j, 1, to_yp], yp)
         rs_send(w, j, 2, T.at[w, j, 7, to_ym], B.at[w, j, 2, to_ym], ym)
         if by_z:
-            rs_send(w, j, 8, T.at[w, j, 5, high], B.at[w, j, 7, high], zp)
-            rs_send(w, j, 9, T.at[w, j, 7, low], B.at[w, j, 7, low], zp)
+            first, last = pl.ds(0, by_z), pl.ds(FFW - by_z, by_z)
+            rs_send(w, j, 8, T.at[w, j, 5, last], B.at[w, j, 7, last], zp)
+            rs_send(w, j, 9, T.at[w, j, 7, first], B.at[w, j, 7, first], zp)
 
     def add(w, j, slot, rows, *held):
         total = T[w, j, slot, rows].astype(jnp.float32)
@@ -236,31 +245,33 @@
         rs_send(w, j, 4, T.at[w, j, 2, high], B.at[w, j, 3, high], ym)
 
     def rs_two_z(w, j):
+        by_z = RS_Z.get((w, j), 0)
         rs[w, j, 1].wait_recv()
         rs[w, j, 2].wait_recv()
-        if (w, j) in BY_Z_RS:
-            add(w, j, 4, low, 1)
-            add(w, j, 4, high, 2)
-        else:
-            add(w, j, 4, full, 1, 2)
-        rs_send(w, j, 5, T.at[w, j, 4], B.at[w, j, 4], zp)
+        if by_z:
+            add(w, j, 4, pl.ds(0, by_z), 1)
+            add(w, j, 4, pl.ds(FFW - by_z, by_z), 2)
+        if by_z < HALF_F:
+            add(w, j, 4, pl.ds(by_z, FFW - 2 * by_z), 1, 2)
+        rs_send(w, j, 5, T.at[w, j, 4], home(w, j, 4), zp)
 
     def rs_three_a(w, j):
-        if (w, j) in BY_Z_RS:
+        by_z = RS_Z.get((w, j), 0)
+        if by_z:
             rs[w, j, 8].wait_recv()
-            add(w, j, 1, high, 7)
+            add(w, j, 1, pl.ds(FFW - by_z, by_z), 7)
             rs[w, j, 9].wait_recv()
-            add(w, j, 3, low, 7)
-        rs_send(w, j, 10, T.at[w, j, 1, high], B.at[w, j, 5, high], yp)
-        rs_send(w, j, 11, T.at[w, j, 3, low], B.at[w, j, 6, low], ym)
+            add(w, j, 3, pl.ds(0, by_z), 7)
+        rs_send(w, j, 10, T.at[w, j, 1, high], home(w, j, 5).at[high], yp)
+        rs_send(w, j, 11, T.at[w, j, 3, low], home(w, j, 6).at[low], ym)
 
     def rs_three_b(w, j):
         rs[w, j, 3].wait_recv()
         add(w, j, 1, low, 3)
-        rs_send(w, j, 6, T.at[w, j, 1, low], B.at[w, j, 5, low], yp)
+        rs_send(w, j, 6, T.at[w, j, 1, low], home(w, j, 5).at[low], yp)
         rs[w, j, 4].wait_recv()
         add(w, j, 3, high, 3)
-        rs_send(w, j, 7, T.at[w, j, 3, high], B.at[w, j, 6, high], ym)
+        rs_send(w, j, 7, T.at[w, j, 3, high], home(w, j, 6).at[high], ym)
 
     def rs_four(w, j):
         for k in (5, 6, 7, 10, 11):
@@ -316,142 +327,158 @@
         o_mom[rows] = new_momentum
         o_anc[rows] = o_anc[rows] - outer_rate * (outer_mean + outer_mu * new_momentum)
 
+    def tail(j):
+        for k in (5, 6, 7, 10, 11):
+            rs[1, j, k].wait_recv()
+
     def down(j):
         rows = pl.ds(j * CH, CH)
         o_acc[rows] = o_acc[rows] + rs_four(1, j)
 
+    ag_own_y(1, 1)
+    ag_own_z(1, 1)
+    up_cast(1)
+    ag_own_y(0, 1)
+    up_cast(0)
+    ag_own_z(0, 1)
+    up_cast(2)
+    x_start()
+    ag_own_z(0, 2)
+    ag_own_y(0, 0)
+    ag_half(0, 1)
+    ag_far(0, 1)
+    ag_own_z(1, 0)
+    ag_own_y(0, 2)
+    ag_half(1, 1)
+    ag_own_z(0, 0)
+    ag_last(0, 1)
+    ag_own_y(1, 0)
+    ag_half(0, 0)
+    ag_half(0, 2)
+    ag_far(0, 0)
+    ag_end(0, 1)
+    x_wait(0)
+    ag_half(1, 0)
+    ag_own_y(1, 2)
+    ag_last(0, 0)
+    forward(0, 1, far)
+    ag_far(0, 2)
+    forward(0, 0, near)
+    ag_far(1, 0)
+    x_wait(1)
+    forward(1, 0, near)
+    forward(0, 1, near)
+    ag_last(0, 2)
+    ag_last(1, 0)
+    ag_half(1, 2)
+    ag_far(1, 1)
+    forward(1, 1, near)
     ag_own_z(1, 2)
-    ag_own_y(1, 1)
-    up_cast(2)
-    up_cast(1)
-    up_cast(0)
-    ag_own_y(0, 0)
-    ag_own_z(0, 2)
-    ag_own_z(0, 1)
-    ag_own_y(0, 1)
-    x_start()
-    ag_own_z(0, 0)
-    ag_own_y(0, 2)
-    ag_own_y(1, 0)
-    ag_far(0, 1)
-    ag_half(0, 0)
-    x_wait(0)
-    ag_half(0, 1)
-    ag_own_y(1, 2)
-    ag_half(0, 2)
-    ag_half(1, 0)
-    ag_own_z(1, 0)
-    forward(0, 1, near)
-    ag_far(0, 0)
-    ag_last(0, 0)
-    ag_last(0, 1)
-    ag_last(0, 2)
-    ag_own_z(1, 1)
-    ag_far(0, 2)
-    ag_half(1, 1)
-    ag_last(1, 0)
-    forward(0, 0, near)
-    ag_end(0, 1)
-    forward(0, 1, far)
-    ag_far(1, 0)
     forward(0, 2, near)
     ag_end(0, 0)
+    ag_end(0, 2)
+    ag_last(1, 1)
+    forward(0, 2, far)
     forward(0, 0, far)
-    ag_end(0, 2)
-    ag_half(1, 2)
-    forward(0, 2, far)
-    x_wait(1)
     swap_partial(0)
-    ag_last(1, 1)
-    forward(1, 0, near)
     partial[0].wait_recv()
+    ag_end(1, 0)
     act()
     swap_hidden(1)
-    ag_far(1, 1)
-    forward(1, 1, near)
+    ag_last(1, 2)
+    forward(1, 0, far)
     hidden[1].wait_recv()
+    ag_far(1, 2)
+    forward(1, 2, near)
+    terms(1, 0)
     terms(1, 1)
-    ag_last(1, 2)
-    ag_far(1, 2)
-    ag_end(1, 0)
-    forward(1, 2, near)
+    rs_three_a(1, 1)
+    rs_one_z(1, 0)
+    ag_end(1, 1)
+    forward(1, 1, far)
+    rs_one_y(1, 1)
     rs_one_z(1, 1)
-    terms(1, 0)
-    ag_end(1, 1)
-    rs_one_z(1, 0)
-    rs_three_a(1, 1)
     rs_one_y(1, 0)
-    forward(1, 1, far)
-    forward(1, 0, far)
     ag_end(1, 2)
     forward(1, 2, far)
     swap_partial(1)
-    rs_one_y(1, 1)
     partial[1].wait_recv()
     grad()
     swap_hidden(0)
     hidden[0].wait_recv()
     terms(0, 2)
+    rs_one_z(0, 2)
     rs_one_y(0, 2)
-    rs_three_a(0, 2)
-    rs_one_z(0, 2)
     terms(0, 1)
+    rs_one_y(0, 1)
     rs_one_z(0, 1)
     terms(0, 0)
-    rs_one_y(0, 1)
+    rs_three_a(0, 2)
     rs_one_z(0, 0)
+    rs_two_z(0, 2)
+    terms(1, 2)
     rs_two_y(0, 2)
     rs_one_y(0, 0)
-    rs_two_z(0, 2)
     rs_two_y(0, 1)
+    rs_three_b(0, 2)
     rs_two_y(0, 0)
-    rs_three_b(0, 2)
-    terms(1, 2)
     rs_three_b(0, 1)
+    rs_two_z(0, 1)
+    rs_two_z(0, 0)
     rs_three_a(0, 1)
-    rs_two_z(0, 1)
-    rs_three_a(0, 0)
-    rs_two_z(0, 0)
-    rs_one_z(1, 2)
-    rs_three_b(0, 0)
-    rs_two_y(1, 1)
-    rs_two_z(1, 1)
-    rs_one_y(1, 2)
-    rs_two_y(1, 0)
-    rs_three_a(1, 0)
     for copy in late:
         copy.wait()
     adam(2)
+    rs_three_a(0, 0)
+    rs_three_b(0, 0)
+    rs_one_z(1, 2)
+    rs_two_z(1, 0)
+    rs_two_y(1, 0)
+    rs_one_y(1, 2)
     adam(1)
+    sum_x(2)
     adam(0)
-    rs_two_z(1, 0)
-    sum_x(2)
+    rs_three_b(1, 0)
+    rs_two_y(1, 1)
     sum_x(1)
+    sum_z(2)
+    rs_three_a(1, 0)
+    rs_two_z(1, 1)
     rs_two_y(1, 2)
+    sum_x(0)
+    rs_three_a(1, 2)
     rs_two_z(1, 2)
+    sum_z(1)
     rs_three_b(1, 1)
-    rs_three_b(1, 0)
-    sum_x(0)
-    sum_z(2)
+    sum_z(0)
     rs_three_b(1, 2)
-    sum_z(1)
-    rs_three_a(1, 2)
+    outer(2)
+    down(0)
+    outer(1)
     down(1)
-    sum_z(0)
-    down(0)
-    outer(2)
-    outer(1)
-    down(2)
     outer(0)
+    tail(2)
     for copy in sends:
         copy.wait_send()
 
 
-def place(anc, mom, m1, m2, acc, o_anc, o_mom, o_m1, o_m2, o_acc, sem):
-    pairs = ((anc, o_anc), (mom, o_mom), (m1, o_m1.at[0]), (m2, o_m2.at[0]), (acc, o_acc.at[0]))
-    copies = [pltpu.make_async_copy(src, dst, sem.at[i]) for i, (src, dst) in enumerate(pairs)]
+def place(anc, mom, m1, m2, acc, E, o_anc, o_mom, o_m1, o_m2, o_acc, S, sem):
+    pairs = ((m1, o_m1.at[0]), (m2, o_m2.at[0]), (acc, o_acc.at[0]), (anc, o_anc), (mom, o_mom))
+    chunk = [pl.ds(j * CH, CH) for j in range(NCH)]
+    copies = [
+        pltpu.make_async_copy(src.at[chunk[j]], dst.at[chunk[j]], sem.at[i, j])
+        for i, (src, dst) in enumerate(pairs)
+        for j in range(NCH)
+        if (i, j) != (2, LAST)
+    ]
     for copy in copies:
         copy.start()
+    total = E[3].astype(jnp.float32)
+    for k in range(3):
+        total += E[k].astype(jnp.float32)
+    S[...] = acc[chunk[LAST]] + total.T
+    copies.append(pltpu.make_async_copy(S, o_acc.at[0, chunk[LAST]], sem.at[2, LAST]))
+    copies[-1].start()
     for copy in copies:
         copy.wait()
 
@@ -463,9 +490,9 @@
     bf16, f32 = jnp.bfloat16, jnp.float32
     held = pl.pallas_call(
         kernel,
-        out_shape=(pltpu.VMEM((ROWS, FFW), f32),) * 5,
+        out_shape=(pltpu.VMEM((ROWS, FFW), f32),) * 5 + (pltpu.VMEM((4, FFW, CH), bf16),),
         in_specs=[pl.BlockSpec(memory_space=pl.ANY)] * 9,
-        out_specs=[pl.BlockSpec(memory_space=pltpu.VMEM)] * 5,
+        out_specs=[pl.BlockSpec(memory_space=pltpu.VMEM)] * 6,
         scratch_shapes=[
             pltpu.VMEM((2, 8, 2 * TOK, ROWS), bf16),
             pltpu.VMEM((2, 8, ROWS, FFW), bf16),
@@ -497,18 +524,18 @@
         ],
         name="window",
         compiler_params=pltpu.CompilerParams(
-            collective_id=0, has_side_effects=True, vmem_limit_bytes=52 * 2**20
+            collective_id=0, has_side_effects=True, vmem_limit_bytes=50 * 2**20
         ),
         cost_estimate=pl.CostEstimate(flops=9_700_000_000, bytes_accessed=30_000_000, transcendentals=200_000),
     )(tokens, cotangent, inner_up, adam_first, adam_second, inner_down, down_accum, anchor_up, outer_momentum)
     return pl.pallas_call(
         place,
         out_shape=(flat, flat, deep, deep, deep),
-        in_specs=[pl.BlockSpec(memory_space=pltpu.VMEM)] * 5,
+        in_specs=[pl.BlockSpec(memory_space=pltpu.VMEM)] * 6,
         out_specs=[pl.BlockSpec(memory_space=pl.ANY)] * 5,
-        scratch_shapes=[dma((5,))],
+        scratch_shapes=[pltpu.VMEM((CH, FFW), f32), dma((5, NCH))],
         name="place",
-        compiler_params=pltpu.CompilerParams(vmem_limit_bytes=2**20),
+        compiler_params=pltpu.CompilerParams(vmem_limit_bytes=4 * 2**20),
     )(*(pltpu.with_memory_space_constraint(value, pltpu.VMEM) for value in held))
 
 

time: 137 us -> 135 us (0.985)
  Pallas kernels: 137 us -> 134 us
    pallas_call x1, Pallas kernels: 134 us -> 132 us  [on_device(): pl.pallas_call(kernel, out_shape=(pltpu.VMEM((ROWS, FFW), f32),) * 5 + (p...]
where the time goes in v4:
time: 135 us
  Pallas kernels  134 us (99%)
    pallas_call x1, Pallas kernels, on_device(): pl.pallas_call(kernel, out_shape=(pltpu.VMEM((ROWS, FFW), f32),) * 5 + (p...  132 us

profile of v4, /device:TPU:0, one launch (start us, length us, event | category | flops | bytes accessed | tf_op | source)
XLA Modules:
  0.0 135.0 jit_solution(7394567801251387655)
XLA Ops:
  0.6 131.7 %window.1 = (f32[768,384]{1,0:T(8,128)S(1)}, f32[768,384]{1,0:T(8,128)S(1)}, f32[768,384]{1,0:T(8,128)S(1)}, f32[768,384]{1,0:T(8,128)S(1)}, f32[768,384]{1,0:T(8,128)S(1)}, /*index=5*/bf16[4,384,256]{2,1,0:T(8,128)(2,1)S(1)}) custom-call(bf16[1,256,12288]{2,1,0:T(8,128)(2,1)} %tok.1, bf16[1,256,12288]{2,1,0:T(8,128)(2,1)} %cot.1, f32[1,768,384]{2,1,0:T(8,128)} %up.1, ...), custom_call_target="tpu_custom_call" | custom-call | flops 9699999744 | bytes 30000000 | tf_op jit(solution)/shard_map/window/pallas_call | solution.py:491
  132.4 2.7 %place.1 = (f32[768,384]{1,0:T(8,128)}, f32[768,384]{1,0:T(8,128)}, f32[1,768,384]{2,1,0:T(8,128)}, f32[1,768,384]{2,1,0:T(8,128)}, f32[1,768,384]{2,1,0:T(8,128)}) custom-call(f32[768,384]{1,0:T(8,128)S(1)} %get-tuple-element.11.anc, f32[768,384]{1,0:T(8,128)S(1)} %get-tuple-element.12.mom, f32[768,384]{1,0:T(8,128)S(1)} %get-tuple-element.13.m1, ...), custom_call_target="tpu_custom_call" | custom-call | tf_op jit(solution)/shard_map/place/pallas_call | solution.py:531

commit v5 on v4

--- a/solution.py
+++ b/solution.py
@@ -438,6 +438,7 @@
     adam(1)
     sum_x(2)
     adam(0)
+    early = len(sends)
     rs_three_b(1, 0)
     rs_two_y(1, 1)
     sum_x(1)
@@ -452,13 +453,15 @@
     rs_three_b(1, 1)
     sum_z(0)
     rs_three_b(1, 2)
+    for copy in sends[:early]:
+        copy.wait_send()
     outer(2)
     down(0)
     outer(1)
     down(1)
     outer(0)
     tail(2)
-    for copy in sends:
+    for copy in sends[early:]:
         copy.wait_send()
 
 

time: 135 us -> 135 us (level)
  no operation moved by 1% of the time
where the time goes in v5:
time: 135 us
  Pallas kernels  134 us (99%)
    pallas_call x1, Pallas kernels, on_device(): pl.pallas_call(kernel, out_shape=(pltpu.VMEM((ROWS, FFW), f32),) * 5 + (p...  132 us

profile of v5, /device:TPU:0, one launch (start us, length us, event | category | flops | bytes accessed | tf_op | source)
XLA Modules:
  0.0 134.8 jit_solution(10929773134652124766)
XLA Ops:
  0.6 131.5 %window.1 = (f32[768,384]{1,0:T(8,128)S(1)}, f32[768,384]{1,0:T(8,128)S(1)}, f32[768,384]{1,0:T(8,128)S(1)}, f32[768,384]{1,0:T(8,128)S(1)}, f32[768,384]{1,0:T(8,128)S(1)}, /*index=5*/bf16[4,384,256]{2,1,0:T(8,128)(2,1)S(1)}) custom-call(bf16[1,256,12288]{2,1,0:T(8,128)(2,1)} %tok.1, bf16[1,256,12288]{2,1,0:T(8,128)(2,1)} %cot.1, f32[1,768,384]{2,1,0:T(8,128)} %up.1, ...), custom_call_target="tpu_custom_call" | custom-call | flops 9699999744 | bytes 30000000 | tf_op jit(solution)/shard_map/window/pallas_call | solution.py:494
  132.2 2.7 %place.1 = (f32[768,384]{1,0:T(8,128)}, f32[768,384]{1,0:T(8,128)}, f32[1,768,384]{2,1,0:T(8,128)}, f32[1,768,384]{2,1,0:T(8,128)}, f32[1,768,384]{2,1,0:T(8,128)}) custom-call(f32[768,384]{1,0:T(8,128)S(1)} %get-tuple-element.11.anc, f32[768,384]{1,0:T(8,128)S(1)} %get-tuple-element.12.mom, f32[768,384]{1,0:T(8,128)S(1)} %get-tuple-element.13.m1, ...), custom_call_target="tpu_custom_call" | custom-call | tf_op jit(solution)/shard_map/place/pallas_call | solution.py:534
